TPU v7x, 128 devices: a whole 4x4x4 slice. The times are simulated.
128 devices in a mesh: lon: 32 (over z, y, x_hi), lat: 4 (over x_lo, core).
Axes of the slice: x: 4 (x_hi: 2, x_lo: 2; x = x_hi * 2 + x_lo), y: 4, z: 4, core: 2. Of those that a mesh axis runs over, the one named last changes fastest.
Arguments:
- noise: bfloat16 [2, 4, 4096, 8192], P(None, None, 'lat', 'lon'), may hold values from -6 to 6
- factors: bfloat16 [9, 32, 256, 256], P(None, 'lat'), may hold values from -0.125 to 0.125
- tile_mask: int32 [9, 32, 2, 2], P(None, 'lat'), may hold values 0 or 1
- lat_weights: float32 [5, 4096], P(None, 'lat'), may hold values from 0.2 to 1
Outputs:
- result_field: float32 [2, 4, 4096, 8192], P(None, None, 'lat', 'lon')
All inputs are finite; a program needn't handle non-finite values. No bound on the sum of `tile_mask` on one device may be relied on, other than what follows from the above.
Results may differ from a plain program's by a relative error of at most 0.0003.
Values may be sent and summed in bfloat16 or wider, within the bound.
No kernel may reach another device: no remote copies, remote signals or barrier semaphores. Data moves between devices by JAX's collectives and lax.ppermute only.
A program may use at most 192 MiB of HBM per device.

v0:
```python
import jax
import jax.numpy as jnp
from jax import lax
from jax.sharding import PartitionSpec as P

TILE = 128
RIM = 2


def shifted_2(block, axis, distance):
    devices = range(lax.axis_size(axis))
    route = [((i - distance) % len(devices), i) for i in devices]
    return lax.ppermute(block, axis, route)


def with_halo(block, sides, width):
    for axis, dim in sides:
        count = lax.axis_size(axis)
        forward = [(i, i + 1) for i in range(count - 1)]
        backward = [(target, source) for source, target in forward]
        low = lax.ppermute(
            lax.slice_in_dim(block, block.shape[dim] - width, None, axis=dim), axis, forward
        )
        high = lax.ppermute(lax.slice_in_dim(block, 0, width, axis=dim), axis, backward)
        block = jnp.concatenate([low, block, high], axis=dim)
    return block


def per_device(noise, factors, tile_mask, lat_weights):
    members, levels, lat_rows, lon_cols = noise.shape
    lag_count, band_count = (factors.shape[0], factors.shape[1])
    tile_count = lon_cols // TILE
    band_rows = lat_rows // band_count
    tile_ones = tile_mask.astype(jnp.bfloat16)
    blocks = (
        factors.reshape(lag_count, band_count, tile_count, TILE, tile_count, TILE)
        * tile_ones[:, :, :, None, :, None]
    ).reshape(lag_count, band_count, lon_cols, lon_cols)
    max_offset = lag_count // 2

    def apply_lag(source, lag_index):
        grouped = source.reshape(members, levels, band_count, band_rows, lon_cols)
        product = jnp.einsum(
            "mvbyj,bji->mvbyi", grouped, blocks[lag_index], preferred_element_type=jnp.float32
        )
        return product.reshape(members, levels, lat_rows, lon_cols)

    mixture = apply_lag(noise, max_offset)
    for offset in [value for value in range(-max_offset, max_offset + 1) if value != 0]:
        shifted = shifted_2(noise, "lon", -offset)
        mixture = mixture + apply_lag(shifted, offset + max_offset)
    padded = with_halo(mixture, (("lat", 2),), RIM)
    result_field = lat_weights[0][None, None, :, None] * padded[:, :, 0:lat_rows]
    for row_shift in range(1, 2 * RIM + 1):
        result_field = (
            result_field
            + lat_weights[row_shift][None, None, :, None]
            * padded[:, :, row_shift : row_shift + lat_rows]
        )
    return result_field


def solution(mesh):
    return jax.shard_map(
        per_device,
        mesh=mesh,
        in_specs=(
            P(None, None, "lat", "lon"),
            P(None, "lat", None, None),
            P(None, "lat", None, None),
            P(None, "lat"),
        ),
        out_specs=P(None, None, "lat", "lon"),
        check_vma=False,
    )
```

profile of v0, /device:TPU:1, one launch (start us, length us, event | category | flops | bytes accessed | tf_op | source)
XLA Modules:
  0.0 591.9 jit_solution(5683715275335050079)
XLA Ops:
  0.0 0.0 copy-start.5
  0.0 9.7 %collective-permute-start.6 = (bf16[2,4,1024,256]{3,2,1,0:T(8,128)(2,1)}, bf16[2,4,1024,256]{3,2,1,0:T(8,128)(2,1)}, u32[]{:S(2)}, u32[]{:S(2)}) collective-permute-start(bf16[2,4,1024,256]{3,2,1,0:T(8,128)(2,1)} %param.4), channel_id=1, source_target_pairs={{12,0},{16,4},{20,8},{24,12},{28,16},{32,20},{36,24},{40,28},{44,3... | collective-permute-start | bytes 12582920 | tf_op jit(solution)/shard_map/ppermute | solution.py:13
  9.7 0.8 collective-permute-start.5
  10.5 0.0 collective-permute-start.4
  10.5 3.0 collective-permute-start.3
  13.4 0.7 collective-permute-start.2
  14.1 13.9 %reshape.76 = bf16[9,8,2,128,2,128]{5,4,3,2,1,0:T(2,128)(2,1)} reshape(bf16[9,8,256,256]{3,2,1,0:T(8,128)(2,1)} %param.5) | data formatting | bytes 18874368 | tf_op jit(solution)/shard_map/reshape | solution.py:36
  28.0 0.0 copy-done.5
  28.0 0.2 copy.7
  28.3 10.9 %broadcast_multiply_fusion = bf16[9,8,2,128,2,128]{5,4,3,2,1,0:T(2,128)(2,1)S(1)} fusion(bf16[9,8,2,128,2,128]{5,4,3,2,1,0:T(2,128)(2,1)} %reshape.76, bf16[9,8,2,2]{3,2,1,0:T(2,128)(2,1)S(1)} %copy.7), kind=kLoop, calls=%fused_computation.17 | loop fusion | flops 4718592 | bytes 18874944 | tf_op jit(solution)/shard_map/mul | solution.py:36
  39.1 60.1 %collective-permute-done.6 = bf16[2,4,1024,256]{3,2,1,0:T(8,128)(2,1)} collective-permute-done((bf16[2,4,1024,256]{3,2,1,0:T(8,128)(2,1)}, bf16[2,4,1024,256]{3,2,1,0:T(8,128)(2,1)}, u32[]{:S(2)}, u32[]{:S(2)}) %collective-permute-start.6) | collective-permute-done | bytes 4194336 | tf_op jit(solution)/shard_map/ppermute | solution.py:13
  99.2 1.8 collective-permute-start.1
  101.0 88.9 %collective-permute-done.5 = bf16[2,4,1024,256]{3,2,1,0:T(8,128)(2,1)} collective-permute-done((bf16[2,4,1024,256]{3,2,1,0:T(8,128)(2,1)}, bf16[2,4,1024,256]{3,2,1,0:T(8,128)(2,1)}, u32[]{:S(2)}, u32[]{:S(2)}) %collective-permute-start.5) | collective-permute-done | bytes 4194336 | tf_op jit(solution)/shard_map/ppermute | solution.py:13
  189.9 0.0 collective-permute-start
  189.9 8.5 %fusion.39 = (bf16[1,8,2,128,2,128]{5,4,3,2,1,0:T(2,128)(2,1)S(1)}, bf16[1,8,2,128,2,128]{5,4,3,2,1,0:T(2,128)(2,1)}, bf16[1,8,2,128,2,128]{5,4,3,2,1,0:T(2,128)...) fusion(bf16[9,8,2,128,2,128]{5,4,3,2,1,0:T(2,128)(2,1)S(1)} %br, ...), kind=kLoop, calls=%fused_computation.45 | loop fusion | bytes 18874368 | tf_op jit(solution)/shard_map/slice | solution.py:44
  198.5 2.5 reshape.94
  201.0 0.0 collective-permute-done.4
  201.0 5.1 collective-permute-start.7
  206.1 7.0 %fusion.26 = f32[8,256,2,4,128]{1,4,3,2,0:T(8,128)} fusion(bf16[2,4,8,128,256]{4,3,2,1,0:T(8,128)(2,1)} %bitcast.2, bf16[8,256,256,1,1]{2,1,0,3,4:T(8,128)(2,1)} %reshape.94), kind=kOutput, calls=%fused_computation.34 | convolution fusion | flops 1073741824 | bytes 13631488 | tf_op jit(solution)/shard_map/mvbyj,bji->mvbyi/dot_general | solution.py:43
  213.1 2.5 reshape.101
  215.6 2.5 reshape.100
  218.1 2.5 reshape.99
  220.7 2.5 reshape.98
  223.2 2.5 reshape.97
  225.7 1.5 reshape.96
  227.2 1.5 reshape.95
  228.7 0.9 reshape.102
  229.6 7.2 %fusion.12 = f32[8,256,2,4,128]{1,4,3,2,0:T(8,128)} fusion(bf16[2,4,8,128,256]{4,3,2,1,0:T(8,128)(2,1)} %bitcast.16, bf16[8,256,256,1,1]{2,1,0,3,4:T(8,128)(2,1)} %reshape.101), kind=kOutput, calls=%fused_computation.20 | convolution fusion | flops 1073741824 | bytes 13631488 | tf_op jit(solution)/shard_map/mvbyj,bji->mvbyi/dot_general | solution.py:43
  236.7 0.0 copy-start.4
  236.7 7.1 %fusion.14 = f32[8,256,2,4,128]{1,4,3,2,0:T(8,128)} fusion(bf16[2,4,8,128,256]{4,3,2,1,0:T(8,128)(2,1)} %bitcast.14, bf16[8,256,256,1,1]{2,1,0,3,4:T(8,128)(2,1)} %reshape.100), kind=kOutput, calls=%fused_computation.22 | convolution fusion | flops 1073741824 | bytes 13631488 | tf_op jit(solution)/shard_map/mvbyj,bji->mvbyi/dot_general | solution.py:43
  243.8 0.0 copy-start.3
  243.8 0.0 copy-done.4
  243.8 6.8 %fusion.16 = f32[8,256,2,4,128]{1,4,3,2,0:T(8,128)} fusion(bf16[2,4,8,128,256]{4,3,2,1,0:T(8,128)(2,1)} %bitcast.12, bf16[8,256,256,1,1]{2,1,0,3,4:T(8,128)(2,1)S(1)} %copy-done.4), kind=kOutput, calls=%fused_computation.24 | convolution fusion | flops 1073741824 | bytes 13631488 | tf_op jit(solution)/shard_map/mvbyj,bji->mvbyi/dot_general | solution.py:43
  250.6 0.0 copy-start.2
  250.6 29.4 %collective-permute-done.3 = bf16[2,4,1024,256]{3,2,1,0:T(8,128)(2,1)} collective-permute-done((bf16[2,4,1024,256]{3,2,1,0:T(8,128)(2,1)}, bf16[2,4,1024,256]{3,2,1,0:T(8,128)(2,1)}, u32[]{:S(2)}, u32[]{:S(2)}) %collective-permute-start.3) | collective-permute-done | bytes 4194336 | tf_op jit(solution)/shard_map/ppermute | solution.py:13
  280.0 0.0 copy-done.3
  280.0 6.7 %fusion.18 = f32[8,256,2,4,128]{1,4,3,2,0:T(8,128)} fusion(bf16[2,4,8,128,256]{4,3,2,1,0:T(8,128)(2,1)} %bitcast.10, bf16[8,256,256,1,1]{2,1,0,3,4:T(8,128)(2,1)S(1)} %copy-done.3), kind=kOutput, calls=%fused_computation.26 | convolution fusion | flops 1073741824 | bytes 13631488 | tf_op jit(solution)/shard_map/mvbyj,bji->mvbyi/dot_general | solution.py:43
  286.7 0.0 copy-start.1
  286.7 0.0 collective-permute-done.2
  286.7 0.0 copy-done.2
  286.7 6.8 %fusion.20 = f32[8,256,2,4,128]{1,4,3,2,0:T(8,128)} fusion(bf16[2,4,8,128,256]{4,3,2,1,0:T(8,128)(2,1)} %bitcast.8, bf16[8,256,256,1,1]{2,1,0,3,4:T(8,128)(2,1)S(1)} %copy-done.2), kind=kOutput, calls=%fused_computation.28 | convolution fusion | flops 1073741824 | bytes 13631488 | tf_op jit(solution)/shard_map/mvbyj,bji->mvbyi/dot_general | solution.py:43
  293.5 0.0 copy-start
  293.5 76.3 %collective-permute-done.1 = bf16[2,4,1024,256]{3,2,1,0:T(8,128)(2,1)} collective-permute-done((bf16[2,4,1024,256]{3,2,1,0:T(8,128)(2,1)}, bf16[2,4,1024,256]{3,2,1,0:T(8,128)(2,1)}, u32[]{:S(2)}, u32[]{:S(2)}) %collective-permute-start.1) | collective-permute-done | bytes 4194336 | tf_op jit(solution)/shard_map/ppermute | solution.py:13
  369.8 0.0 copy-done.1
  369.8 6.7 %fusion.22 = f32[8,256,2,4,128]{1,4,3,2,0:T(8,128)} fusion(bf16[2,4,8,128,256]{4,3,2,1,0:T(8,128)(2,1)} %bitcast.6, bf16[8,256,256,1,1]{2,1,0,3,4:T(8,128)(2,1)S(1)} %copy-done.1), kind=kOutput, calls=%fused_computation.30 | convolution fusion | flops 1073741824 | bytes 13631488 | tf_op jit(solution)/shard_map/mvbyj,bji->mvbyi/dot_general | solution.py:43
  376.5 84.3 %collective-permute-done = bf16[2,4,1024,256]{3,2,1,0:T(8,128)(2,1)} collective-permute-done((bf16[2,4,1024,256]{3,2,1,0:T(8,128)(2,1)}, bf16[2,4,1024,256]{3,2,1,0:T(8,128)(2,1)}, u32[]{:S(2)}, u32[]{:S(2)}) %collective-permute-start) | collective-permute-done | bytes 4194336 | tf_op jit(solution)/shard_map/ppermute | solution.py:13
  460.8 0.0 copy-done
  460.8 6.7 %fusion.24 = f32[8,256,2,4,128]{1,4,3,2,0:T(8,128)} fusion(bf16[2,4,8,128,256]{4,3,2,1,0:T(8,128)(2,1)} %bitcast.4, bf16[8,256,256,1,1]{2,1,0,3,4:T(8,128)(2,1)S(1)} %copy-done), kind=kOutput, calls=%fused_computation.32 | convolution fusion | flops 1073741824 | bytes 13631488 | tf_op jit(solution)/shard_map/mvbyj,bji->mvbyi/dot_general | solution.py:43
  467.5 81.6 %collective-permute-done.7 = bf16[2,4,1024,256]{3,2,1,0:T(8,128)(2,1)} collective-permute-done((bf16[2,4,1024,256]{3,2,1,0:T(8,128)(2,1)}, bf16[2,4,1024,256]{3,2,1,0:T(8,128)(2,1)}, u32[]{:S(2)}, u32[]{:S(2)}) %collective-permute-start.7) | collective-permute-done | bytes 4194336 | tf_op jit(solution)/shard_map/ppermute | solution.py:13
  549.0 22.6 %add_bitcast_fusion = f32[2,4,8,128,256]{4,3,1,0,2:T(8,128)S(1)} fusion(f32[8,256,2,4,128]{1,4,3,2,0:T(8,128)} %fusion.12, f32[8,256,2,4,128]{1,4,3,2,0:T(8,128)} %fusion.14, f32[8,256,2,4,128]{1,4,3,2,0:T(8,128)} %fusion.16, f32[8,256,2,4,128]{1,4,3,2,0:T(8,128)} %fusion.18, f32[8,256,2,4,128]{1,4,3,2,0:T(8,128)} %fusion.20, ...), kind=kOutput, calls=%fused_computation.16 | convolution fusion | flops 1090519040 | bytes 80740352 | tf_op jit(solution)/shard_map/mvbyj,bji->mvbyi/dot_general | solution.py:43
  571.6 0.0 copy-start.6
  571.6 0.6 copy.17
  572.3 3.7 collective-permute-start.8
  576.0 1.9 collective-permute-start.9
  577.9 0.0 copy-done.6
  578.0 0.0 collective-permute-done.8
  578.0 3.1 collective-permute-done.9
  581.1 10.9 %fusion.3 = f32[2,4,1024,256]{3,2,1,0:T(8,128)} fusion(f32[2,4,1024,256]{3,2,1,0:T(8,128)S(1)} %bitcast.47, f32[2,4,2,256]{3,2,1,0:T(2,128)S(1)} %collective-permute-done.9, f32[2,4,2,256]{3,2,1,0:T(2,128)S(1)} %collective-permute-done.8, f32[1024]{0:T(1024)S(1)} %bitcast.51, f32[1024]{0:T(1024)S(1)} %bitcast.52, f32[1024]{0:T(1024)S(1)} %bitcast.49, ...), kind=kLoop, calls=%fused_computation.7 | loop fusion | flops 27262976 | bytes 16830464 | tf_op jit(solution)/shard_map/add | solution.py:56
  (3 shorter events, 0.0 us)
Async XLA Ops:
  0.0 28.0 %copy-start.5 = (s32[9,8,2,2]{0,3,2,1:T(2,128)S(1)}, s32[9,8,2,2]{0,3,2,1:T(2,128)}, u32[]{:S(2)}) copy-start(s32[9,8,2,2]{0,3,2,1:T(2,128)} %param.6) | copy-start | bytes 3460
  0.0 99.2 %collective-permute-start.6 = (bf16[2,4,1024,256]{3,2,1,0:T(8,128)(2,1)}, bf16[2,4,1024,256]{3,2,1,0:T(8,128)(2,1)}, u32[]{:S(2)}, u32[]{:S(2)}) collective-permute-start(bf16[2,4,1024,256]{3,2,1,0:T(8,128)(2,1)} %param.4), channel_id=1, source_target_pairs={{12,0},{16,4},{20,8},{24,12},{28,16},{32,20},{36,24},{40,28},{44,3... | collective-permute-start | bytes 12582920 | tf_op jit(solution)/shard_map/ppermute | solution.py:13
  9.7 180.3 %collective-permute-start.5 = (bf16[2,4,1024,256]{3,2,1,0:T(8,128)(2,1)}, bf16[2,4,1024,256]{3,2,1,0:T(8,128)(2,1)}, u32[]{:S(2)}, u32[]{:S(2)}) collective-permute-start(bf16[2,4,1024,256]{3,2,1,0:T(8,128)(2,1)} %param.4), channel_id=1, source_target_pairs={{8,0},{12,4},{16,8},{20,12},{24,16},{28,20},{32,24},{36,28},{40,32... | collective-permute-start | bytes 12582920 | tf_op jit(solution)/shard_map/ppermute | solution.py:13
  10.5 190.6 %collective-permute-start.4 = (bf16[2,4,1024,256]{3,2,1,0:T(8,128)(2,1)}, bf16[2,4,1024,256]{3,2,1,0:T(8,128)(2,1)}, u32[]{:S(2)}, u32[]{:S(2)}) collective-permute-start(bf16[2,4,1024,256]{3,2,1,0:T(8,128)(2,1)} %param.4), channel_id=1, source_target_pairs={{4,0},{8,4},{12,8},{16,12},{20,16},{24,20},{28,24},{32,28},{36,32}... | collective-permute-start | bytes 12582920 | tf_op jit(solution)/shard_map/ppermute | solution.py:13
  10.5 269.5 %collective-permute-start.3 = (bf16[2,4,1024,256]{3,2,1,0:T(8,128)(2,1)}, bf16[2,4,1024,256]{3,2,1,0:T(8,128)(2,1)}, u32[]{:S(2)}, u32[]{:S(2)}) collective-permute-start(bf16[2,4,1024,256]{3,2,1,0:T(8,128)(2,1)} %param.4), channel_id=1, source_target_pairs={{124,0},{0,4},{4,8},{8,12},{12,16},{16,20},{20,24},{24,28},{28,32}... | collective-permute-start | bytes 12582920 | tf_op jit(solution)/shard_map/ppermute | solution.py:13
  13.4 273.3 %collective-permute-start.2 = (bf16[2,4,1024,256]{3,2,1,0:T(8,128)(2,1)}, bf16[2,4,1024,256]{3,2,1,0:T(8,128)(2,1)}, u32[]{:S(2)}, u32[]{:S(2)}) collective-permute-start(bf16[2,4,1024,256]{3,2,1,0:T(8,128)(2,1)} %param.4), channel_id=1, source_target_pairs={{120,0},{124,4},{0,8},{4,12},{8,16},{12,20},{16,24},{20,28},{24,32... | collective-permute-start | bytes 12582920 | tf_op jit(solution)/shard_map/ppermute | solution.py:13
  99.2 270.6 %collective-permute-start.1 = (bf16[2,4,1024,256]{3,2,1,0:T(8,128)(2,1)}, bf16[2,4,1024,256]{3,2,1,0:T(8,128)(2,1)}, u32[]{:S(2)}, u32[]{:S(2)}) collective-permute-start(bf16[2,4,1024,256]{3,2,1,0:T(8,128)(2,1)} %param.4), channel_id=1, source_target_pairs={{116,0},{120,4},{124,8},{0,12},{4,16},{8,20},{12,24},{16,28},{20,3... | collective-permute-start | bytes 12582920 | tf_op jit(solution)/shard_map/ppermute | solution.py:13
  189.9 270.8 %collective-permute-start = (bf16[2,4,1024,256]{3,2,1,0:T(8,128)(2,1)}, bf16[2,4,1024,256]{3,2,1,0:T(8,128)(2,1)}, u32[]{:S(2)}, u32[]{:S(2)}) collective-permute-start(bf16[2,4,1024,256]{3,2,1,0:T(8,128)(2,1)} %param.4), channel_id=1, source_target_pairs={{112,0},{116,4},{120,8},{124,12},{0,16},{4,20},{8,24},{12,28},{16,... | collective-permute-start | bytes 12582920 | tf_op jit(solution)/shard_map/ppermute | solution.py:13
  201.0 348.0 %collective-permute-start.7 = (bf16[2,4,1024,256]{3,2,1,0:T(8,128)(2,1)}, bf16[2,4,1024,256]{3,2,1,0:T(8,128)(2,1)}, u32[]{:S(2)}, u32[]{:S(2)}) collective-permute-start(bf16[2,4,1024,256]{3,2,1,0:T(8,128)(2,1)} %param.4), channel_id=1, source_target_pairs={{16,0},{20,4},{24,8},{28,12},{32,16},{36,20},{40,24},{44,28},{48,3... | collective-permute-start | bytes 12582920 | tf_op jit(solution)/shard_map/ppermute | solution.py:13
  236.7 7.1 %copy-start.4 = (bf16[8,256,256,1,1]{2,1,0,3,4:T(8,128)(2,1)S(1)}, bf16[8,256,256,1,1]{2,1,0,3,4:T(8,128)(2,1)}, u32[]{:S(2)}) copy-start(bf16[8,256,256,1,1]{2,1,0,3,4:T(8,128)(2,1)} %reshape.99) | copy-start | bytes 3145732
  243.8 36.2 %copy-start.3 = (bf16[8,256,256,1,1]{2,1,0,3,4:T(8,128)(2,1)S(1)}, bf16[8,256,256,1,1]{2,1,0,3,4:T(8,128)(2,1)}, u32[]{:S(2)}) copy-start(bf16[8,256,256,1,1]{2,1,0,3,4:T(8,128)(2,1)} %reshape.98) | copy-start | bytes 3145732
  250.6 36.1 %copy-start.2 = (bf16[8,256,256,1,1]{2,1,0,3,4:T(8,128)(2,1)S(1)}, bf16[8,256,256,1,1]{2,1,0,3,4:T(8,128)(2,1)}, u32[]{:S(2)}) copy-start(bf16[8,256,256,1,1]{2,1,0,3,4:T(8,128)(2,1)} %reshape.97) | copy-start | bytes 3145732
  286.7 83.1 %copy-start.1 = (bf16[8,256,256,1,1]{2,1,0,3,4:T(8,128)(2,1)S(1)}, bf16[8,256,256,1,1]{2,1,0,3,4:T(8,128)(2,1)}, u32[]{:S(2)}) copy-start(bf16[8,256,256,1,1]{2,1,0,3,4:T(8,128)(2,1)} %reshape.96) | copy-start | bytes 3145732
  293.5 167.3 %copy-start = (bf16[8,256,256,1,1]{2,1,0,3,4:T(8,128)(2,1)S(1)}, bf16[8,256,256,1,1]{2,1,0,3,4:T(8,128)(2,1)}, u32[]{:S(2)}) copy-start(bf16[8,256,256,1,1]{2,1,0,3,4:T(8,128)(2,1)} %reshape.95) | copy-start | bytes 3145732
  571.6 6.3 %copy-start.6 = (f32[5,1024]{1,0:T(8,128)S(1)}, f32[5,1024]{1,0:T(8,128)}, u32[]{:S(2)}) copy-start(f32[5,1024]{1,0:T(8,128)} %param.7) | copy-start | bytes 61444
  572.3 5.7 collective-permute-start.8
  576.0 5.1 collective-permute-start.9
where the time goes:
time: 593 us; the launch traced here: 592 us
  waiting for transfers between devices  424 us (72%)
  matrix products  77.4 us (13%)
  local copies, waits for them, and re-layouts  42.3 us (7%)
  starting transfers between devices  26.6 us (4%)
  other arithmetic  21.7 us (4%)
    ppermute x8, waiting for transfers between devices, shifted_2(): return lax.ppermute(block, axis, route)  421 us
    dot_general x9, matrix products, apply_lag(): jnp.einsum('mvbyj,bji->mvbyi', grouped, blocks[lag_index], preferred_elem...  77.4 us
    ppermute x8, starting transfers between devices, shifted_2(): return lax.ppermute(block, axis, route)  21 us
    squeeze x9, local copies, waits for them, and re-layouts, apply_lag(): blocks[lag_index]  19 us
    reshape x1, local copies, waits for them, and re-layouts, per_device(): factors.reshape(lag_count, band_count, tile_count, TILE, tile_count, TILE)  13.9 us
  transfers between devices with their start and end apart: 10, of which 7 were waited for; matrix products, arithmetic and copies ran while one was open for 18% of the time, Pallas kernels for 0%

commit v1 on v0

v1 whole, which is shorter than its diff:
```python
import functools

import jax
import jax.numpy as jnp
from jax import lax
from jax.experimental import pallas as pl
from jax.experimental.pallas import tpu as pltpu
from jax.sharding import PartitionSpec as P

TILE = 128
RIM = 2
TOP = 32767.0
PACK = 16


def mix_kernel(bands, quarter, mask_ref, noise_ref, factors_ref, out_ref, weights):
    lags, _, width, _ = factors_ref.shape
    count, rows, _ = noise_ref.shape
    reach = lags // 2
    band = pl.program_id(0)
    tiles = width // TILE
    local_band = quarter[0] * pl.num_programs(0) + band
    for lag in range(lags):
        for a in range(tiles):
            for b in range(tiles):
                place = ((lag * bands + local_band) * tiles + a) * tiles + b
                keep = mask_ref[place].astype(jnp.float32).astype(jnp.bfloat16)
                weights[pl.ds(lag * width + a * TILE, TILE), pl.ds(b * TILE, TILE)] = (
                    factors_ref[lag, 0, pl.ds(a * TILE, TILE), pl.ds(b * TILE, TILE)] * keep
                )

    @pl.loop(0, count)
    def _(c):
        total = jnp.zeros((rows, width), jnp.float32)
        for lag in range(lags):
            source = lax.rem(c + (lag - reach) + count, count)
            total += jnp.dot(
                noise_ref[source],
                weights[pl.ds(lag * width, width), :],
                preferred_element_type=jnp.float32,
            )
        peak = jnp.maximum(jnp.max(jnp.abs(total), axis=0, keepdims=True), 2.0**-120)
        power = jnp.ceil(jnp.log2(peak) + 1e-5)
        coded = jnp.round(total * jnp.exp2(-power) * TOP)
        out_ref[c, pl.ds(0, rows), :] = coded.astype(jnp.int32).astype(jnp.int16)
        out_ref[c, pl.ds(rows, PACK), :] = (
            jnp.broadcast_to(power, (PACK, width)).astype(jnp.int32).astype(jnp.int16)
        )


def mix(quarter, mask, noise, factors):
    count, rows, width = noise.shape
    lags, bands = factors.shape[:2]
    parts = rows // TILE
    return pl.pallas_call(
        functools.partial(mix_kernel, bands),
        out_shape=jax.ShapeDtypeStruct((count, parts, TILE + PACK, width), jnp.int16),
        grid_spec=pltpu.PrefetchScalarGridSpec(
            num_scalar_prefetch=2,
            grid=(parts,),
            in_specs=[
                pl.BlockSpec((count, TILE, width), lambda b, quarter, mask: (0, b, 0)),
                pl.BlockSpec(
                    (lags, 1, width, width),
                    lambda b, quarter, mask: (0, quarter[0] * parts + b, 0, 0),
                ),
            ],
            out_specs=pl.BlockSpec(
                (count, None, TILE + PACK, width), lambda b, quarter, mask: (0, b, 0, 0)
            ),
            scratch_shapes=[pltpu.VMEM((lags * width, width), jnp.bfloat16)],
        ),
        compiler_params=pltpu.CompilerParams(vmem_limit_bytes=48 * 2**20),
    )(quarter, mask, noise, factors)


def filter_kernel(coded_ref, low_ref, high_ref, lat_weights_ref, out_ref, padded, spread):
    blocks, _, width = coded_ref.shape
    rows = out_ref.shape[0]
    taps = spread.shape[0]

    @pl.when(pl.program_id(0) == 0)
    def _():
        for tap in range(taps):
            spread[tap] = jnp.broadcast_to(lat_weights_ref[:, tap : tap + 1], spread.shape[1:])

    padded[pl.ds(0, 8), :] = low_ref[...]
    padded[pl.ds(8 + rows, 8), :] = high_ref[...]
    for block in range(blocks):
        power = coded_ref[block, pl.ds(TILE, PACK), :].astype(jnp.float32)[0:1]
        scale = jnp.exp2(power) * (1.0 / TOP)
        padded[pl.ds(8 + block * TILE, TILE), :] = (
            coded_ref[block, pl.ds(0, TILE), :].astype(jnp.float32) * scale
        )
    for block in range(blocks):
        for half in range(width // TILE):
            lanes = pl.ds(half * TILE, TILE)
            total = jnp.zeros((TILE, TILE), jnp.float32)
            for tap in range(taps):
                total += (
                    spread[tap, pl.ds(block * TILE, TILE), :]
                    * padded[pl.ds(8 - RIM + tap + block * TILE, TILE), lanes]
                )
            out_ref[pl.ds(block * TILE, TILE), lanes] = total


def band_filter(coded, low, high, lat_weights):
    fields, blocks, _, width = coded.shape
    rows = blocks * TILE
    taps = lat_weights.shape[0]
    return pl.pallas_call(
        filter_kernel,
        out_shape=jax.ShapeDtypeStruct((fields, rows, width), jnp.float32),
        grid=(fields,),
        in_specs=[
            pl.BlockSpec((None, blocks, TILE + PACK, width), lambda f: (f, 0, 0, 0)),
            pl.BlockSpec((None, 8, width), lambda f: (f, 0, 0)),
            pl.BlockSpec((None, 8, width), lambda f: (f, 0, 0)),
            pl.BlockSpec((rows, taps), lambda f: (0, 0)),
        ],
        out_specs=pl.BlockSpec((None, rows, width), lambda f: (f, 0, 0)),
        scratch_shapes=[
            pltpu.VMEM((rows + 16, width), jnp.float32),
            pltpu.VMEM((taps, rows, TILE), jnp.float32),
        ],
        compiler_params=pltpu.CompilerParams(vmem_limit_bytes=48 * 2**20),
    )(coded, low, high, lat_weights.T)


def edge(coded, block, start):
    scale = jnp.exp2(coded[:, block, TILE : TILE + 1].astype(jnp.float32)) * (1.0 / TOP)
    return coded[:, block, start : start + RIM].astype(jnp.float32) * scale


def per_device(noise, factors, tile_mask, lat_weights):
    members, levels, rows, width = noise.shape
    fields = members * levels
    count = lax.axis_size("lon")
    quarters = count // fields
    quarter = (lax.axis_index("lon") % quarters).astype(jnp.int32).reshape(1)
    mine = lax.all_to_all(
        noise.reshape(count, rows // quarters, width), "lon", 0, 0, tiled=True
    )
    sent = mix(quarter, tile_mask.reshape(-1), mine, factors)
    coded = lax.all_to_all(sent, "lon", 0, 0, tiled=True)
    coded = coded.reshape(fields, rows // TILE, TILE + PACK, width)
    lat = lax.axis_size("lat")
    forward = [(i, i + 1) for i in range(lat - 1)]
    backward = [(i + 1, i) for i in range(lat - 1)]
    low = lax.ppermute(edge(coded, -1, TILE - RIM), "lat", forward)
    high = lax.ppermute(edge(coded, 0, 0), "lat", backward)
    low = jnp.pad(low, ((0, 0), (8 - RIM, 0), (0, 0)))
    high = jnp.pad(high, ((0, 0), (0, 8 - RIM), (0, 0)))
    result_field = band_filter(coded, low, high, lat_weights)
    return result_field.reshape(members, levels, rows, width)


def solution(mesh):
    return jax.shard_map(
        per_device,
        mesh=mesh,
        in_specs=(
            P(None, None, "lat", "lon"),
            P(None, "lat", None, None),
            P(None, "lat", None, None),
            P(None, "lat"),
        ),
        out_specs=P(None, None, "lat", "lon"),
        check_vma=False,
    )
```

time: 593 us -> 186 us (0.31)
  waiting for transfers between devices: 424 us -> 57.2 us
  matrix products: 77.4 us -> 0 us
  blocking collectives: 0 us -> 68.2 us
  local copies, waits for them, and re-layouts: 42.3 us -> 5.13 us
  Pallas kernels: 0 us -> 36.3 us
  other arithmetic: 21.7 us -> 0.05 us
  starting transfers between devices: 26.6 us -> 18.2 us
    ppermute x10 -> x2, waiting for transfers between devices: 424 us -> 2.86 us  [the longest x1 2.86 us: per_device(): high = lax.ppermute(edge(coded, 0, 0), 'lat', backward)]
    dot_general x9 -> x0, matrix products: 77.4 us -> none  [apply_lag(): jnp.einsum('mvbyj,bji->mvbyi', grouped, blocks[lag_index], preferred_elem...]
    all_to_all x0 -> x1, blocking collectives: none -> 68.2 us  [per_device(): coded = lax.all_to_all(sent, 'lon', 0, 0, tiled=True)]
    all_to_all x0 -> x1, waiting for transfers between devices: none -> 54.3 us  [per_device(): lax.all_to_all(noise.reshape(count, rows // quarters, width), 'lon', 0, 0...]
    pallas_call x0 -> x2, Pallas kernels: none -> 36.3 us  [the longest x1 28.1 us: mix(): pl.pallas_call(functools.partial(mix_kernel, bands), out_shape=jax.ShapeD...]
    ppermute x10 -> x2, starting transfers between devices: 26.6 us -> 6.58 us  [the longest x1 4.66 us: per_device(): low = lax.ppermute(edge(coded, -1, TILE - RIM), 'lat', forward)]
    squeeze x9 -> x0, local copies, waits for them, and re-layouts: 19 us -> none  [apply_lag(): blocks[lag_index]]
    reshape x1, local copies, waits for them, and re-layouts: 13.9 us -> 0.15 us  [per_device(): sent = mix(quarter, tile_mask.reshape(-1), mine, factors)]
  transfers between devices with their start and end apart: 10 -> 3, of which waited for: 7 -> 2; matrix products, arithmetic and copies ran while one was open for 18% -> 0% of each run, Pallas kernels for 0% -> 0%
where the time goes in v1:
time: 186 us; the launch traced here: 185 us
  blocking collectives  68.2 us (37%)
  waiting for transfers between devices  57.2 us (31%)
  Pallas kernels  36.3 us (20%)
  starting transfers between devices  18.2 us (10%)
  local copies, waits for them, and re-layouts  5.13 us (3%)
    all_to_all x1, blocking collectives, per_device(): coded = lax.all_to_all(sent, 'lon', 0, 0, tiled=True)  68.2 us
    all_to_all x1, waiting for transfers between devices, per_device(): lax.all_to_all(noise.reshape(count, rows // quarters, width), 'lon', 0, 0...  54.3 us
    pallas_call x1, Pallas kernels, mix(): pl.pallas_call(functools.partial(mix_kernel, bands), out_shape=jax.ShapeD...  28.1 us
    all_to_all x1, starting transfers between devices, per_device(): lax.all_to_all(noise.reshape(count, rows // quarters, width), 'lon', 0, 0...  11.6 us
    pallas_call x1, Pallas kernels, band_filter(): pl.pallas_call(filter_kernel, out_shape=jax.ShapeDtypeStruct((fields, row...  8.16 us
    unnamed x10, local copies, waits for them, and re-layouts  4.95 us
    ppermute x1, starting transfers between devices, per_device(): low = lax.ppermute(edge(coded, -1, TILE - RIM), 'lat', forward)  4.66 us
  transfers between devices with their start and end apart: 3, of which 2 were waited for; matrix products, arithmetic and copies ran while one was open for 0% of the time, Pallas kernels for 0%

profile of v1, /device:TPU:1, one launch (start us, length us, event | category | flops | bytes accessed | tf_op | source)
XLA Modules:
  0.0 185.2 jit_solution(5759891898589396500)
XLA Ops:
  0.0 0.0 copy-start.3
  0.0 11.6 %all-to-all-start = ((bf16[32,256,256]{2,1,0:T(8,128)(2,1)}), bf16[32,256,256]{2,1,0:T(8,128)(2,1)}, u32[]{:S(2)}, u32[]{:S(2)}) async-start(bf16[32,256,256]{2,1,0:T(8,128)(2,1)} %bitcast.27), calls=%async_computation | async-start | bytes 8388608 | tf_op jit(solution)/shard_map/all_to_all | solution.py:141
  11.6 0.0 copy-done.3
  11.6 0.2 copy.11
  11.8 0.1 reshape.58.mask_ref
  12.0 54.3 %all-to-all-done.noise_ref = bf16[32,256,256]{2,1,0:T(8,128)(2,1)} async-done(((bf16[32,256,256]{2,1,0:T(8,128)(2,1)}), bf16[32,256,256]{2,1,0:T(8,128)(2,1)}, u32[]{:S(2)}, u32[]{:S(2)}) %all-to-all-start) | async-done | bytes 4194336 | tf_op jit(solution)/shard_map/all_to_all | solution.py:141
  66.3 28.1 %shard_map.46 = s16[32,2,144,256]{3,2,1,0:T(8,128)(2,1)} custom-call(s32[1]{0:T(128)} %bitcast.quarter, s32[288]{0:T(512)S(1)} %reshape.58.mask_ref, bf16[32,256,256]{2,1,0:T(8,128)(2,1)} %all-to-all-done.noise_ref, bf16[9,8,256,256]{3,2,1,0:T(8,128)(2,1)} %factors_ref.1), custom_call_target="tpu_custom_call" | custom-call | tf_op jit(solution)/shard_map/pallas_call | solution.py:55
  94.4 0.0 copy-start.2
  94.5 68.2 %all_to_all.10 = s16[32,2,144,256]{3,2,1,0:T(8,128)(2,1)S(1)} all-to-all(s16[32,2,144,256]{3,2,1,0:T(8,128)(2,1)} %shard_map.46), channel_id=1, replica_groups=mesh['lon'=32,'lat'=4] {'lon'}, dimensions={0} | all-to-all | bytes 9437184 | tf_op jit(solution)/shard_map/all_to_all | solution.py:145
  162.8 0.0 copy-start
  162.8 2.2 %copy-done = s16[32,2,144,256]{3,2,1,0:T(8,128)(2,1)} copy-done((s16[32,2,144,256]{3,2,1,0:T(8,128)(2,1)}, s16[32,2,144,256]{3,2,1,0:T(8,128)(2,1)S(1)}, u32[]{:S(2)}) %copy-start) | copy-done | bytes 4718616
  164.9 4.7 %collective-permute-start = (f32[8,2,256]{2,1,0:T(2,128)S(1)}, f32[8,2,256]{2,1,0:T(2,128)S(1)}, u32[]{:S(2)}, u32[]{:S(2)}) collective-permute-start(f32[8,2,256]{2,1,0:T(2,128)S(1)} %get-tuple-element.6), channel_id=1, source_target_pairs={{0,1},{1,2},{2,3},{4,5},{5,6},{6,7},{8,9},{9,10},{10,11},{12,13},{... | collective-permute-start | bytes 49160 | tf_op jit(solution)/shard_map/ppermute | solution.py:150
  169.6 1.9 %collective-permute-start.1 = (f32[8,2,256]{2,1,0:T(2,128)S(1)}, f32[8,2,256]{2,1,0:T(2,128)S(1)}, u32[]{:S(2)}, u32[]{:S(2)}) collective-permute-start(f32[8,2,256]{2,1,0:T(2,128)S(1)} %get-tuple-element.5), channel_id=1, source_target_pairs={{1,0},{2,1},{3,2},{5,4},{6,5},{7,6},{9,8},{10,9},{11,10},{13,12},{... | collective-permute-start | bytes 49160 | tf_op jit(solution)/shard_map/ppermute | solution.py:151
  171.5 0.0 copy-done.2
  171.6 0.2 copy.16
  171.8 0.0 collective-permute-done
  171.8 2.9 %collective-permute-done.1 = f32[8,2,256]{2,1,0:T(2,128)S(1)} collective-permute-done((f32[8,2,256]{2,1,0:T(2,128)S(1)}, f32[8,2,256]{2,1,0:T(2,128)S(1)}, u32[]{:S(2)}, u32[]{:S(2)}) %collective-permute-start.1) | collective-permute-done | bytes 16416 | tf_op jit(solution)/shard_map/ppermute | solution.py:151
  174.7 0.0 copy-start.1
  174.7 2.3 %copy-done.1 = s16[32,2,144,256]{3,2,1,0:T(8,128)(2,1)S(1)} copy-done((s16[32,2,144,256]{3,2,1,0:T(8,128)(2,1)S(1)}, s16[32,2,144,256]{3,2,1,0:T(8,128)(2,1)}, u32[]{:S(2)}) %copy-start.1) | copy-done | bytes 4718616
  177.0 8.2 %shard_map.47 = f32[8,1024,256]{2,1,0:T(8,128)} custom-call(s16[8,8,144,256]{3,2,1,0:T(8,128)(2,1)S(1)} %bitcast.25, f32[8,8,256]{2,1,0:T(8,128)S(1)} %pad.8.low_ref, f32[8,8,256]{2,1,0:T(8,128)S(1)} %pad.9.high_ref, f32[1024,5]{1,0:T(8,128)S(1)} %bitcast.26), custom_call_target="tpu_custom_call" | custom-call | tf_op jit(solution)/shard_map/pallas_call | solution.py:111
  (5 shorter events, 0.1 us)
Async XLA Ops:
  0.0 11.6 %copy-start.3 = (s32[9,8,2,2]{0,3,2,1:T(2,128)S(1)}, s32[9,8,2,2]{0,3,2,1:T(2,128)}, u32[]{:S(2)}) copy-start(s32[9,8,2,2]{0,3,2,1:T(2,128)} %param.6) | copy-start | bytes 3460
  0.0 66.3 %all-to-all-start = ((bf16[32,256,256]{2,1,0:T(8,128)(2,1)}), bf16[32,256,256]{2,1,0:T(8,128)(2,1)}, u32[]{:S(2)}, u32[]{:S(2)}) async-start(bf16[32,256,256]{2,1,0:T(8,128)(2,1)} %bitcast.27), calls=%async_computation | async-start | bytes 8388608 | tf_op jit(solution)/shard_map/all_to_all | solution.py:141
  94.4 77.1 %copy-start.2 = (f32[5,1024]{1,0:T(8,128)S(1)}, f32[5,1024]{1,0:T(8,128)}, u32[]{:S(2)}) copy-start(f32[5,1024]{1,0:T(8,128)} %param.7) | copy-start | bytes 61444
  162.8 2.2 %copy-start = (s16[32,2,144,256]{3,2,1,0:T(8,128)(2,1)}, s16[32,2,144,256]{3,2,1,0:T(8,128)(2,1)S(1)}, u32[]{:S(2)}) copy-start(s16[32,2,144,256]{3,2,1,0:T(8,128)(2,1)S(1)} %all_to_all.10) | copy-start | bytes 14155780
  164.9 6.8 %collective-permute-start = (f32[8,2,256]{2,1,0:T(2,128)S(1)}, f32[8,2,256]{2,1,0:T(2,128)S(1)}, u32[]{:S(2)}, u32[]{:S(2)}) collective-permute-start(f32[8,2,256]{2,1,0:T(2,128)S(1)} %get-tuple-element.6), channel_id=1, source_target_pairs={{0,1},{1,2},{2,3},{4,5},{5,6},{6,7},{8,9},{9,10},{10,11},{12,13},{... | collective-permute-start | bytes 49160 | tf_op jit(solution)/shard_map/ppermute | solution.py:150
  169.6 5.1 %collective-permute-start.1 = (f32[8,2,256]{2,1,0:T(2,128)S(1)}, f32[8,2,256]{2,1,0:T(2,128)S(1)}, u32[]{:S(2)}, u32[]{:S(2)}) collective-permute-start(f32[8,2,256]{2,1,0:T(2,128)S(1)} %get-tuple-element.5), channel_id=1, source_target_pairs={{1,0},{2,1},{3,2},{5,4},{6,5},{7,6},{9,8},{10,9},{11,10},{13,12},{... | collective-permute-start | bytes 49160 | tf_op jit(solution)/shard_map/ppermute | solution.py:151
  174.7 2.3 %copy-start.1 = (s16[32,2,144,256]{3,2,1,0:T(8,128)(2,1)S(1)}, s16[32,2,144,256]{3,2,1,0:T(8,128)(2,1)}, u32[]{:S(2)}) copy-start(s16[32,2,144,256]{3,2,1,0:T(8,128)(2,1)} %copy-done) | copy-start | bytes 14155780

commit v2 on v1

v2 whole, which is shorter than its diff:
```python
import functools

import jax
import jax.numpy as jnp
from jax import lax
from jax.experimental import pallas as pl
from jax.experimental.pallas import tpu as pltpu
from jax.sharding import PartitionSpec as P

TILE = 128
RIM = 2
TOP = 32767.0
SIDE = 16
GROUP = 8


def weights_kernel(place_ref, mask_ref, factors_ref, weights_ref):
    lags, _, width, _ = factors_ref.shape
    tiles = width // TILE
    band = place_ref[0] + pl.program_id(0)
    for lag in range(lags):
        for a in range(tiles):
            for b in range(tiles):
                index = ((lag * place_ref[1] + band) * tiles + a) * tiles + b
                keep = mask_ref[index].astype(jnp.float32).astype(jnp.bfloat16)
                weights_ref[lag, pl.ds(a * TILE, TILE), pl.ds(b * TILE, TILE)] = (
                    factors_ref[lag, 0, pl.ds(a * TILE, TILE), pl.ds(b * TILE, TILE)] * keep
                )


def masked_weights(place, mask, factors, parts):
    lags, _, width, _ = factors.shape
    return pl.pallas_call(
        weights_kernel,
        out_shape=jax.ShapeDtypeStruct((parts, lags, width, width), factors.dtype),
        grid_spec=pltpu.PrefetchScalarGridSpec(
            num_scalar_prefetch=2,
            grid=(parts,),
            in_specs=[
                pl.BlockSpec(
                    (lags, 1, width, width), lambda b, place, mask: (0, place[0] + b, 0, 0)
                )
            ],
            out_specs=pl.BlockSpec(
                (None, lags, width, width), lambda b, place, mask: (b, 0, 0, 0)
            ),
        ),
        compiler_params=pltpu.CompilerParams(vmem_limit_bytes=12 * 2**20),
    )(place, mask, factors)


def mix_kernel(group, place_ref, noise_ref, weights_ref, coded_ref):
    lags, width, _ = weights_ref.shape
    count, rows, _ = noise_ref.shape
    reach = lags // 2
    halves = width // TILE
    step = pl.program_id(1)
    total = None
    for lag in range(lags):
        source = jnp.concatenate(
            [
                noise_ref[lax.rem(step * group + g + (lag - reach) + count, count)]
                for g in range(group)
            ],
            axis=0,
        )
        product = jnp.dot(source, weights_ref[lag], preferred_element_type=jnp.float32)
        total = product if total is None else total + product
    for g in range(group):
        powers, edges = [], []
        for half in range(halves):
            block = total[g * rows : (g + 1) * rows, half * TILE : (half + 1) * TILE]
            peak = jnp.maximum(jnp.max(jnp.abs(block), axis=0, keepdims=True), 2.0**-120)
            power = jnp.ceil(jnp.log2(peak) + 1e-5)
            coded = jnp.round(block * jnp.exp2(-power) * TOP).astype(jnp.int32)
            coded_ref[g, half * rows : (half + 1) * rows, :] = coded.astype(jnp.int16)
            powers.append(power.astype(jnp.int32))
            edges.append(jnp.where(place_ref[3] == 1, coded[rows - RIM :], coded[:RIM]))
        empty = jnp.zeros((SIDE // 2 - halves, TILE), jnp.int32)
        side = powers + [empty] + powers + edges + [empty[: SIDE // 2 - halves * (1 + RIM)]]
        coded_ref[g, halves * rows :, :] = jnp.concatenate(side, axis=0).astype(jnp.int16)


def mix(place, noise, weights):
    count, rows, width = noise.shape
    parts, lags = weights.shape[:2]
    rows = rows // parts
    sent = rows * width // TILE + SIDE
    return pl.pallas_call(
        functools.partial(mix_kernel, GROUP),
        out_shape=jax.ShapeDtypeStruct((count, parts, sent, TILE), jnp.int16),
        grid_spec=pltpu.PrefetchScalarGridSpec(
            num_scalar_prefetch=1,
            grid=(parts, count // GROUP),
            in_specs=[
                pl.BlockSpec((count, rows, width), lambda b, s, place: (0, b, 0)),
                pl.BlockSpec((None, lags, width, width), lambda b, s, place: (b, 0, 0, 0)),
            ],
            out_specs=pl.BlockSpec((GROUP, None, sent, TILE), lambda b, s, place: (s, b, 0, 0)),
        ),
        compiler_params=pltpu.CompilerParams(vmem_limit_bytes=28 * 2**20),
        cost_estimate=pl.CostEstimate(
            flops=2 * lags * count * rows * parts * width * width,
            bytes_accessed=4 * count * rows * parts * width,
            transcendentals=0,
        ),
    )(place, noise, weights)


def filter_kernel(coded_ref, lat_ref, out_ref, padded, spread):
    bands, _, _ = coded_ref.shape
    rows, width = out_ref.shape
    halves = width // TILE
    strip = rows // bands
    taps = spread.shape[0]

    @pl.when(pl.program_id(0) == 0)
    def _():
        for tap in range(taps):
            spread[tap] = jnp.broadcast_to(lat_ref[:, tap : tap + 1], spread.shape[1:])

    for band in range(bands):
        side = coded_ref[band, halves * strip :].astype(jnp.float32)
        for half in range(halves):
            lanes = pl.ds(half * TILE, TILE)
            scale = jnp.exp2(side[half : half + 1]) * (1.0 / TOP)
            padded[pl.ds(8 + band * strip, strip), lanes] = (
                coded_ref[band, half * strip : (half + 1) * strip].astype(jnp.float32) * scale
            )
            if band in (0, bands - 1):
                start = SIDE // 2
                scale = jnp.exp2(side[start + half : start + half + 1]) * (1.0 / TOP)
                start += halves + half * RIM
                place = 8 - RIM if band == 0 else 8 + rows
                padded[place : place + RIM, lanes] = side[start : start + RIM] * scale
    for band in range(bands):
        for half in range(halves):
            lanes = pl.ds(half * TILE, TILE)
            total = jnp.zeros((strip, TILE), jnp.float32)
            for tap in range(taps):
                total += (
                    spread[tap, pl.ds(band * strip, strip), :]
                    * padded[pl.ds(8 - RIM + tap + band * strip, strip), lanes]
                )
            out_ref[pl.ds(band * strip, strip), lanes] = total


def band_filter(coded, lat_weights, width):
    fields, bands, sent, _ = coded.shape
    rows, taps = lat_weights.shape
    return pl.pallas_call(
        filter_kernel,
        out_shape=jax.ShapeDtypeStruct((fields, rows, width), jnp.float32),
        grid=(fields,),
        in_specs=[
            pl.BlockSpec((None, bands, sent, TILE), lambda f: (f, 0, 0, 0)),
            pl.BlockSpec((rows, taps), lambda f: (0, 0)),
        ],
        out_specs=pl.BlockSpec((None, rows, width), lambda f: (f, 0, 0)),
        scratch_shapes=[
            pltpu.VMEM((rows + 16, width), jnp.float32),
            pltpu.VMEM((taps, rows, TILE), jnp.float32),
        ],
        compiler_params=pltpu.CompilerParams(vmem_limit_bytes=20 * 2**20),
        cost_estimate=pl.CostEstimate(
            flops=10 * fields * rows * width,
            bytes_accessed=6 * fields * rows * width,
            transcendentals=0,
        ),
    )(coded, lat_weights)


def per_device(noise, factors, tile_mask, lat_weights):
    members, levels, rows, width = noise.shape
    fields = members * levels
    bands = factors.shape[1]
    count, lat = lax.axis_size("lon"), lax.axis_size("lat")
    strip = rows // bands
    parts = fields * bands // count
    shares = bands // parts
    share = (lax.axis_index("lon") % shares).astype(jnp.int32)
    top = (share == shares - 1).astype(jnp.int32)
    place = jnp.stack([share * parts, jnp.int32(bands), top * (parts - 1), top])
    joins = []
    for field in range(fields):
        for row in range(lat - 1):
            south = (field * shares + shares - 1) * lat + row
            north = field * shares * lat + row + 1
            joins += [(south, north), (north, south)]
    weights = masked_weights(place, tile_mask.reshape(-1), factors, parts)
    mine = lax.all_to_all(
        noise.reshape(count, parts * strip, width), "lon", 0, 0, tiled=True
    )
    lat_weights = lat_weights.T
    mine, weights, lat_weights = lax.optimization_barrier((mine, weights, lat_weights))
    coded = mix(place, mine, weights)
    spot = (0, place[2], coded.shape[2] - SIDE, 0)
    side = lax.dynamic_slice(coded, spot, (count, 1, SIDE, TILE))
    other = lax.ppermute(side, ("lon", "lat"), joins)
    side = jnp.where(jnp.arange(SIDE)[None, None, :, None] < SIDE // 2, side, other)
    coded = lax.dynamic_update_slice(coded, side, spot)
    coded = lax.all_to_all(coded, "lon", 0, 0, tiled=True)
    coded = coded.reshape(fields, bands, -1, TILE)
    result_field = band_filter(coded, lat_weights, width)
    return result_field.reshape(members, levels, rows, width)


def solution(mesh):
    return jax.shard_map(
        per_device,
        mesh=mesh,
        in_specs=(
            P(None, None, "lat", "lon"),
            P(None, "lat", None, None),
            P(None, "lat", None, None),
            P(None, "lat"),
        ),
        out_specs=P(None, None, "lat", "lon"),
        check_vma=False,
    )
```

time: 186 us -> 163 us (0.88); the launches traced: 185 us -> 160 us
  Pallas kernels: 36.3 us -> 23.8 us
  blocking collectives: 68.2 us -> 60.1 us
  waiting for transfers between devices: 57.2 us -> 51.7 us
    pallas_call x1 -> x2, Pallas kernels: 28.1 us -> 15.7 us  [the longest x1 14.4 us: mix(): pl.pallas_call(functools.partial(mix_kernel, GROUP), out_shape=jax.ShapeD...]
    all_to_all x1, blocking collectives: 68.2 us -> 60.1 us  [per_device(): coded = lax.all_to_all(coded, 'lon', 0, 0, tiled=True)]
    all_to_all x1, waiting for transfers between devices: 54.3 us -> 49.1 us  [per_device(): lax.all_to_all(noise.reshape(count, parts * strip, width), 'lon', 0, 0, t...]
    ppermute x2 -> x1, starting transfers between devices: 6.58 us -> 8.06 us  [per_device(): other = lax.ppermute(side, ('lon', 'lat'), joins)]
    unnamed x10 -> x8, local copies, waits for them, and re-layouts: 4.95 us -> 4.12 us
  transfers between devices with their start and end apart: 3 -> 2, of which waited for: 2 -> 2; matrix products, arithmetic and copies ran while one was open for 0% -> 0% of each run, Pallas kernels for 0% -> 1%
where the time goes in v2:
time: 163 us; the launch traced here: 160 us
  blocking collectives  60.1 us (37%)
  waiting for transfers between devices  51.7 us (32%)
  Pallas kernels  23.8 us (15%)
  starting transfers between devices  19.7 us (12%)
  local copies, waits for them, and re-layouts  4.28 us (3%)
    all_to_all x1, blocking collectives, per_device(): coded = lax.all_to_all(coded, 'lon', 0, 0, tiled=True)  60.1 us
    all_to_all x1, waiting for transfers between devices, per_device(): lax.all_to_all(noise.reshape(count, parts * strip, width), 'lon', 0, 0, t...  49.1 us
    pallas_call x1, Pallas kernels, mix(): pl.pallas_call(functools.partial(mix_kernel, GROUP), out_shape=jax.ShapeD...  14.4 us
    all_to_all x1, starting transfers between devices, per_device(): lax.all_to_all(noise.reshape(count, parts * strip, width), 'lon', 0, 0, t...  11.6 us
    pallas_call x1, Pallas kernels, band_filter(): pl.pallas_call(filter_kernel, out_shape=jax.ShapeDtypeStruct((fields, row...  8.14 us
    ppermute x1, starting transfers between devices, per_device(): other = lax.ppermute(side, ('lon', 'lat'), joins)  8.06 us
    unnamed x8, local copies, waits for them, and re-layouts  4.12 us
  transfers between devices with their start and end apart: 2, of which 2 were waited for; matrix products, arithmetic and copies ran while one was open for 0% of the time, Pallas kernels for 1%

profile of v2, /device:TPU:1, one launch (start us, length us, event | category | flops | bytes accessed | tf_op | source)
XLA Modules:
  0.0 159.9 jit_solution(10067412294938405667)
XLA Ops:
  0.0 0.0 copy-start.2
  0.0 0.0 copy-start.1
  0.0 11.6 %all-to-all-start = ((bf16[32,256,256]{2,1,0:T(8,128)(2,1)}), bf16[32,256,256]{2,1,0:T(8,128)(2,1)}, u32[]{:S(2)}, u32[]{:S(2)}) async-start(bf16[32,256,256]{2,1,0:T(8,128)(2,1)} %bitcast.8), calls=%async_computation | async-start | bytes 8388608 | tf_op jit(solution)/shard_map/all_to_all | solution.py:191
  11.6 0.0 copy-done.2
  11.6 0.2 copy.6
  11.8 0.1 reshape.20.mask_ref
  12.0 0.0 copy-done.1
  12.0 0.2 copy.7
  12.2 0.1 pad_add_fusion.place_ref
  12.3 0.0 copy-start
  12.3 3.7 %copy-done = bf16[9,8,256,256]{3,2,1,0:T(8,128)(2,1)S(1)} copy-done((bf16[9,8,256,256]{3,2,1,0:T(8,128)(2,1)S(1)}, bf16[9,8,256,256]{3,2,1,0:T(8,128)(2,1)}, u32[]{:S(2)}) %copy-start) | copy-done | bytes 9437208
  16.0 1.3 shard_map.46.weights_ref
  17.3 49.1 %all-to-all-done.noise_ref = bf16[32,256,256]{2,1,0:T(8,128)(2,1)} async-done(((bf16[32,256,256]{2,1,0:T(8,128)(2,1)}), bf16[32,256,256]{2,1,0:T(8,128)(2,1)}, u32[]{:S(2)}, u32[]{:S(2)}) %all-to-all-start) | async-done | bytes 4194336 | tf_op jit(solution)/shard_map/all_to_all | solution.py:191
  66.3 14.4 %shard_map.47 = s16[32,2,272,128]{3,2,1,0:T(8,128)(2,1)S(1)} custom-call(s32[4]{0:T(128)S(1)} %pad_add_fusion.place_ref, bf16[32,256,256]{2,1,0:T(8,128)(2,1)} %all-to-all-done.noise_ref, bf16[2,9,256,256]{3,2,1,0:T(8,128)(2,1)S(1)} %shard_map.46.weights_ref), custom_call_target="tpu_custom_call" | custom-call | flops 9663676416 | bytes 8388608 | tf_op jit(solution)/shard_map/pallas_call | solution.py:89
  80.8 8.1 %collective-permute-start = (s16[32,1,16,128]{3,2,1,0:T(8,128)(2,1)S(1)}, s16[32,1,16,128]{3,2,1,0:T(8,128)(2,1)S(1)}, u32[]{:S(2)}, u32[]{:S(2)}) collective-permute-start(s16[32,1,16,128]{3,2,1,0:T(8,128)(2,1)S(1)} %constant_dynamic-slice_fusion), channel_id=1, source_target_pairs={{12,1},{1,12},{13,2},{2,13},{14,3},{3,14},{28,17},{17,28},{29,18},... | collective-permute-start | bytes 393224 | tf_op jit(solution)/shard_map/ppermute | solution.py:199
  88.9 2.6 %collective-permute-done = s16[32,1,16,128]{3,2,1,0:T(8,128)(2,1)S(1)} collective-permute-done((s16[32,1,16,128]{3,2,1,0:T(8,128)(2,1)S(1)}, s16[32,1,16,128]{3,2,1,0:T(8,128)(2,1)S(1)}, u32[]{:S(2)}, u32[]{:S(2)}) %collective-permute-start) | collective-permute-done | bytes 131104 | tf_op jit(solution)/shard_map/ppermute | solution.py:199
  91.5 0.1 select_dynamic-update-slice_fusion
  91.6 60.1 %all_to_all.10 = s16[32,2,272,128]{3,2,1,0:T(8,128)(2,1)S(1)} all-to-all(s16[32,2,272,128]{3,2,1,0:T(8,128)(2,1)S(1)} %select_dynamic-update-slice_fusion), channel_id=1, replica_groups=mesh['lon'=32,'lat'=4] {'lon'}, dimensions={0} | all-to-all | bytes 8912896 | tf_op jit(solution)/shard_map/all_to_all | solution.py:202
  151.7 8.1 %shard_map.48 = f32[8,1024,256]{2,1,0:T(8,128)} custom-call(s16[8,8,272,128]{3,2,1,0:T(8,128)(2,1)S(1)} %bitcast.6, f32[1024,5]{1,0:T(8,128)S(1)} %bitcast.7), custom_call_target="tpu_custom_call" | custom-call | flops 20971520 | bytes 12582912 | tf_op jit(solution)/shard_map/pallas_call | solution.py:151
  (2 shorter events, 0.0 us)
Async XLA Ops:
  0.0 11.6 %copy-start.2 = (s32[9,8,2,2]{0,3,2,1:T(2,128)S(1)}, s32[9,8,2,2]{0,3,2,1:T(2,128)}, u32[]{:S(2)}) copy-start(s32[9,8,2,2]{0,3,2,1:T(2,128)} %param.6) | copy-start | bytes 3460
  0.0 12.0 %copy-start.1 = (f32[5,1024]{1,0:T(8,128)S(1)}, f32[5,1024]{1,0:T(8,128)}, u32[]{:S(2)}) copy-start(f32[5,1024]{1,0:T(8,128)} %param.7) | copy-start | bytes 61444
  0.0 66.3 %all-to-all-start = ((bf16[32,256,256]{2,1,0:T(8,128)(2,1)}), bf16[32,256,256]{2,1,0:T(8,128)(2,1)}, u32[]{:S(2)}, u32[]{:S(2)}) async-start(bf16[32,256,256]{2,1,0:T(8,128)(2,1)} %bitcast.8), calls=%async_computation | async-start | bytes 8388608 | tf_op jit(solution)/shard_map/all_to_all | solution.py:191
  12.3 3.7 %copy-start = (bf16[9,8,256,256]{3,2,1,0:T(8,128)(2,1)S(1)}, bf16[9,8,256,256]{3,2,1,0:T(8,128)(2,1)}, u32[]{:S(2)}) copy-start(bf16[9,8,256,256]{3,2,1,0:T(8,128)(2,1)} %factors_ref.1) | copy-start | bytes 28311556
  80.8 10.7 %collective-permute-start = (s16[32,1,16,128]{3,2,1,0:T(8,128)(2,1)S(1)}, s16[32,1,16,128]{3,2,1,0:T(8,128)(2,1)S(1)}, u32[]{:S(2)}, u32[]{:S(2)}) collective-permute-start(s16[32,1,16,128]{3,2,1,0:T(8,128)(2,1)S(1)} %constant_dynamic-slice_fusion), channel_id=1, source_target_pairs={{12,1},{1,12},{13,2},{2,13},{14,3},{3,14},{28,17},{17,28},{29,18},... | collective-permute-start | bytes 393224 | tf_op jit(solution)/shard_map/ppermute | solution.py:199

commit v3 on v0

v3 whole, which is shorter than its diff:
```python
import functools

import jax
import jax.numpy as jnp
from jax import lax
from jax.experimental import pallas as pl
from jax.experimental.pallas import tpu as pltpu
from jax.sharding import PartitionSpec as P

TILE = 128
RIM = 2
TOP = 32767.0
SIDE = 16
GROUP = 8


def device_at(place):
    return ((place // 8 + place // 2) % 4) * 8 + place % 8


def place_of(device):
    return ((device // 8 + 4 - device // 2 % 4) % 4) * 8 + device % 8


def code(block):
    peak = jnp.maximum(jnp.max(jnp.abs(block), axis=0, keepdims=True), 2.0**-120)
    power = jnp.ceil(jnp.log2(peak) + 1e-5)
    return jnp.round(block * jnp.exp2(-power) * TOP).astype(jnp.int32), power.astype(jnp.int32)


def fill_places(places, count, reach):
    for index in range(count + 2 * reach):
        places[index] = place_of((index + count - reach) % count)


def banded(places, noise_ref, weights, start, group, lines):
    lags = len(weights)
    targets = [device_at(start + g) for g in range(group)]
    total = None
    for lag in range(lags):
        blocks = [noise_ref[places[target + lag], lines, :] for target in targets]
        product = jnp.dot(
            jnp.concatenate(blocks, axis=0), weights[lag][...], preferred_element_type=jnp.float32
        )
        total = product if total is None else total + product
    return total


def rim_kernel(
    shares, mask_ref, noise_ref, factors_ref, side_ref, weights_ref, loaded, sems, places
):
    parts, lags, width, _ = weights_ref.shape
    count, rows, _ = noise_ref.shape
    tiles = width // TILE
    share = place_of(lax.axis_index("lon")) % shares
    last = share == shares - 1
    copies = [
        pltpu.make_async_copy(
            factors_ref.at[:, share * parts + part], loaded.at[part], sems.at[part]
        )
        for part in range(parts)
    ]
    for copy in copies:
        copy.start()
    fill_places(places, count, lags // 2)
    for part in range(parts):
        copies[part].wait()
        for lag in range(lags):
            for a in range(tiles):
                for b in range(tiles):
                    keep = mask_ref[share * parts + part, a, b, lag]
                    keep = keep.astype(jnp.float32).astype(jnp.bfloat16)
                    spot = (pl.ds(a * TILE, TILE), pl.ds(b * TILE, TILE))
                    weights_ref[(part, lag, *spot)] = loaded[(part, lag, *spot)] * keep
    weights = [weights_ref.at[jnp.where(last, parts - 1, 0), lag] for lag in range(lags)]
    line = pl.multiple_of(jnp.where(last, rows - SIDE, 0), SIDE)
    total = banded(places, noise_ref, weights, 0, count, pl.ds(line, SIDE))
    for g in range(count):
        block = total[g * SIDE : (g + 1) * SIDE]
        edge = jnp.where(last, block[SIDE - RIM :], block[:RIM])
        powers, codes = [], []
        for half in range(width // TILE):
            coded, power = code(edge[:, half * TILE : (half + 1) * TILE])
            powers.append(power)
            codes.append(coded)
        empty = jnp.zeros((SIDE - 3 * len(codes), TILE), jnp.int32)
        side_ref[g] = jnp.concatenate([empty] + powers + codes, axis=0).astype(jnp.int16)


def rim(mask, noise, factors, parts, shares):
    count, _, width = noise.shape
    lags = factors.shape[0]
    vmem = pl.BlockSpec(memory_space=pltpu.VMEM)
    held = (parts, lags, width, width)
    return pl.pallas_call(
        functools.partial(rim_kernel, shares),
        out_shape=[
            jax.ShapeDtypeStruct((count, SIDE, TILE), jnp.int16),
            jax.ShapeDtypeStruct(held, factors.dtype),
        ],
        in_specs=[
            pl.BlockSpec(memory_space=pltpu.SMEM),
            vmem,
            pl.BlockSpec(memory_space=pltpu.HBM),
        ],
        out_specs=[vmem] * 2,
        scratch_shapes=[
            pltpu.VMEM(held, factors.dtype),
            pltpu.SemaphoreType.DMA((parts,)),
            pltpu.SMEM((count + lags - 1,), jnp.int32),
        ],
        compiler_params=pltpu.CompilerParams(vmem_limit_bytes=46 * 2**20),
        cost_estimate=pl.CostEstimate(
            flops=2 * lags * count * SIDE * width * width,
            bytes_accessed=4 * count * SIDE * width,
            transcendentals=0,
        ),
    )(mask, noise, factors)


def mix_kernel(noise_ref, weights_ref, coded_ref, powers, places):
    parts, lags, width, _ = weights_ref.shape
    count, rows, _ = noise_ref.shape
    strip = rows // parts
    group = powers.shape[0] // parts
    halves = width // TILE
    part, step = pl.program_id(1), pl.program_id(0)

    @pl.when((part == 0) & (step == 0))
    def _():
        fill_places(places, count, lags // 2)

    weights = [weights_ref.at[part, lag] for lag in range(lags)]
    lines = pl.ds(pl.multiple_of(part * strip, strip), strip)
    total = banded(places, noise_ref, weights, step * group, group, lines)
    for g in range(group):
        block = total[g * strip : (g + 1) * strip]
        for half in range(halves):
            coded, power = code(block[:, half * TILE : (half + 1) * TILE])
            start = pl.multiple_of((part * halves + half) * strip, strip)
            coded_ref[step * group + g, pl.ds(start, strip), :] = coded.astype(jnp.int16)
            powers[part * group + g, half : half + 1, :] = power

    @pl.when(part == parts - 1)
    def _():
        for g in range(group):
            side = [powers[p * group + g, :halves] for p in range(parts)]
            side.append(jnp.zeros((SIDE - parts * halves, TILE), jnp.int32))
            coded_ref[step * group + g, parts * halves * strip :, :] = jnp.concatenate(side, axis=0).astype(
                jnp.int16
            )


def mix(noise, weights):
    count, rows, width = noise.shape
    parts, lags = weights.shape[:2]
    strip = rows // parts
    sent = rows * width // TILE + SIDE
    return pl.pallas_call(
        mix_kernel,
        out_shape=jax.ShapeDtypeStruct((count, sent, TILE), jnp.int16),
        grid=(count // GROUP, parts),
        in_specs=[pl.BlockSpec(memory_space=pltpu.VMEM)] * 2,
        out_specs=pl.BlockSpec(memory_space=pltpu.VMEM),
        scratch_shapes=[
            pltpu.VMEM((parts * GROUP, 8, TILE), jnp.int32),
            pltpu.SMEM((count + lags - 1,), jnp.int32),
        ],
        compiler_params=pltpu.CompilerParams(vmem_limit_bytes=16 * 2**20),
        cost_estimate=pl.CostEstimate(
            flops=2 * lags * count * rows * width * width,
            bytes_accessed=4 * count * rows * width,
            transcendentals=0,
        ),
    )(noise, weights)


def filter_kernel(parts, coded_ref, lat_ref, out_ref, padded, spread):
    shares, _, _ = coded_ref.shape
    rows, width = out_ref.shape
    halves = width // TILE
    held = rows // shares
    strip = held // parts
    taps = spread.shape[0]

    @pl.when(pl.program_id(0) == 0)
    def _():
        empty = jnp.zeros((8 - taps, TILE), jnp.float32)
        for start in range(0, rows, TILE):
            lines = slice(start, start + TILE)
            columns = jnp.concatenate([lat_ref[:, lines], empty], axis=0).T
            for tap in range(taps):
                spread[tap, lines, :] = jnp.broadcast_to(columns[:, tap : tap + 1], (TILE, TILE))

    for share in range(shares):
        side = coded_ref[share, halves * held :].astype(jnp.float32)
        for half in range(halves):
            lanes = slice(half * TILE, (half + 1) * TILE)
            for part in range(parts):
                line = part * halves + half
                scale = jnp.exp2(side[line : line + 1]) * (1.0 / TOP)
                place = 8 + share * held + part * strip
                padded[place : place + strip, lanes] = (
                    coded_ref[share, line * strip : (line + 1) * strip].astype(jnp.float32) * scale
                )
            if share in (0, shares - 1):
                line = SIDE - 3 * halves
                scale = jnp.exp2(side[line + half : line + half + 1]) * (1.0 / TOP)
                line += halves + half * RIM
                place = 8 - RIM if share == 0 else 8 + rows
                padded[place : place + RIM, lanes] = side[line : line + RIM] * scale
    for start in range(0, rows, strip):
        for half in range(halves):
            lanes = slice(half * TILE, (half + 1) * TILE)
            total = None
            for tap in range(taps):
                place = 8 - RIM + tap + start
                term = spread[tap, start : start + strip] * padded[place : place + strip, lanes]
                total = term if total is None else total + term
            out_ref[start : start + strip, lanes] = total


def band_filter(coded, lat_weights, parts, width):
    fields, shares, sent, _ = coded.shape
    taps, rows = lat_weights.shape
    return pl.pallas_call(
        functools.partial(filter_kernel, parts),
        out_shape=jax.ShapeDtypeStruct((fields, rows, width), jnp.float32),
        grid=(fields,),
        in_specs=[
            pl.BlockSpec((None, shares, sent, TILE), lambda f: (f, 0, 0, 0)),
            pl.BlockSpec((taps, rows), lambda f: (0, 0)),
        ],
        out_specs=pl.BlockSpec((None, rows, width), lambda f: (f, 0, 0)),
        scratch_shapes=[
            pltpu.VMEM((rows + 16, width), jnp.float32),
            pltpu.VMEM((taps, rows, TILE), jnp.float32),
        ],
        compiler_params=pltpu.CompilerParams(vmem_limit_bytes=12 * 2**20),
        cost_estimate=pl.CostEstimate(
            flops=10 * fields * rows * width,
            bytes_accessed=6 * fields * rows * width,
            transcendentals=0,
        ),
    )(coded, lat_weights)


def per_device(noise, factors, tile_mask, lat_weights):
    members, levels, rows, width = noise.shape
    fields = members * levels
    bands = factors.shape[1]
    count, lat = lax.axis_size("lon"), lax.axis_size("lat")
    parts = fields * bands // count
    shares = bands // parts
    held = rows // shares
    groups = [[device_at(place) for place in range(count)]]
    joins = []
    for field in range(fields):
        for row in range(lat - 1):
            south = groups[0][field * shares + shares - 1] * lat + row
            north = groups[0][field * shares] * lat + row + 1
            joins += [(south, north), (north, south)]
    mine = lax.all_to_all(
        noise.reshape(count, held, width), "lon", 0, 0, axis_index_groups=groups, tiled=True
    )
    edges, weights = rim(tile_mask.transpose(1, 2, 3, 0), mine, factors, parts, shares)
    other = lax.ppermute(edges, ("lon", "lat"), joins)
    coded = mix(mine, weights)
    own = SIDE - 3 * (width // TILE)
    side = jnp.concatenate([coded[:, -SIDE : own - SIDE], other[:, own:]], axis=1)
    coded = lax.dynamic_update_slice(coded, side, (0, coded.shape[1] - SIDE, 0))
    coded = lax.all_to_all(coded, "lon", 0, 0, axis_index_groups=groups, tiled=True)
    result_field = band_filter(
        coded.reshape(fields, shares, -1, TILE), lat_weights, parts, width
    )
    return result_field.reshape(members, levels, rows, width)


def solution(mesh):
    return jax.shard_map(
        per_device,
        mesh=mesh,
        in_specs=(
            P(None, None, "lat", "lon"),
            P(None, "lat", None, None),
            P(None, "lat", None, None),
            P(None, "lat"),
        ),
        out_specs=P(None, None, "lat", "lon"),
        check_vma=False,
    )
```

time: 593 us -> 154 us (0.26)
  waiting for transfers between devices: 424 us -> 0.01 us
  blocking collectives: 0 us -> 122 us
  matrix products: 77.4 us -> 0 us
  local copies, waits for them, and re-layouts: 42.3 us -> 0.04 us
  Pallas kernels: 0 us -> 23.8 us
  other arithmetic: 21.7 us -> 0.06 us
  starting transfers between devices: 26.6 us -> 5.71 us
    ppermute x10 -> x1, waiting for transfers between devices: 424 us -> 0.01 us  [per_device(): other = lax.ppermute(edges, ('lon', 'lat'), joins)]
    all_to_all x0 -> x2, blocking collectives: none -> 122 us  [the longest x1 62.1 us: per_device(): lax.all_to_all(noise.reshape(count, held, width), 'lon', 0, 0, axis_index...]
    dot_general x9 -> x0, matrix products: 77.4 us -> none  [apply_lag(): jnp.einsum('mvbyj,bji->mvbyi', grouped, blocks[lag_index], preferred_elem...]
    pallas_call x0 -> x3, Pallas kernels: none -> 23.8 us  [the longest x1 11.9 us: mix(): pl.pallas_call(mix_kernel, out_shape=jax.ShapeDtypeStruct((count, sent, T...]
    ppermute x10 -> x1, starting transfers between devices: 26.6 us -> 5.71 us  [per_device(): other = lax.ppermute(edges, ('lon', 'lat'), joins)]
    squeeze x9 -> x0, local copies, waits for them, and re-layouts: 19 us -> none  [apply_lag(): blocks[lag_index]]
    reshape x1 -> x0, local copies, waits for them, and re-layouts: 13.9 us -> none  [per_device(): factors.reshape(lag_count, band_count, tile_count, TILE, tile_count, TILE)]
    mul x1 -> x0, other arithmetic: 10.9 us -> none  [per_device(): factors.reshape(lag_count, band_count, tile_count, TILE, tile_count, TILE)]
  transfers between devices with their start and end apart: 10 -> 1, of which waited for: 7 -> 0; matrix products, arithmetic and copies ran while one was open for 18% -> 0% of each run, Pallas kernels for 0% -> 8%
where the time goes in v3:
time: 154 us; the launch traced here: 152 us
  blocking collectives  122 us (79%)
  Pallas kernels  23.8 us (15%)
  starting transfers between devices  5.71 us (4%)
    all_to_all x1, blocking collectives, per_device(): lax.all_to_all(noise.reshape(count, held, width), 'lon', 0, 0, axis_index...  62.1 us
    all_to_all x1, blocking collectives, per_device(): lax.all_to_all(coded, 'lon', 0, 0, axis_index_groups=groups, tiled=True)  60.1 us
    pallas_call x1, Pallas kernels, mix(): pl.pallas_call(mix_kernel, out_shape=jax.ShapeDtypeStruct((count, sent, T...  11.9 us
    pallas_call x1, Pallas kernels, band_filter(): pl.pallas_call(functools.partial(filter_kernel, parts), out_shape=jax.Sha...  8.42 us
    ppermute x1, starting transfers between devices, per_device(): other = lax.ppermute(edges, ('lon', 'lat'), joins)  5.71 us
    pallas_call x1, Pallas kernels, rim(): pl.pallas_call(functools.partial(rim_kernel, shares), out_shape=[jax.Shap...  3.51 us
  transfers between devices with their start and end apart: 1, of which 0 were waited for; matrix products, arithmetic and copies ran while one was open for 0% of the time, Pallas kernels for 8%

profile of v3, /device:TPU:1, one launch (start us, length us, event | category | flops | bytes accessed | tf_op | source)
XLA Modules:
  0.0 151.9 jit_solution(10870696977885563620)
XLA Ops:
  0.0 0.0 copy-start.1
  0.0 62.1 %all_to_all.10.noise_ref = bf16[32,256,256]{2,1,0:T(8,128)(2,1)S(1)} all-to-all(bf16[32,256,256]{2,1,0:T(8,128)(2,1)} %bitcast.6), channel_id=1, replica_groups={{0,4,40,44,80,84,120,124,32,36,72,76,112,116,24,28,64,68,104,108,16,20,..., dimensions={0} | all-to-all | bytes 8388608 | tf_op jit(solution)/shard_map/all_to_all | solution.py:263
  62.1 0.0 copy-done.1
  62.1 3.5 %shard_map.46 = (s16[32,16,128]{2,1,0:T(8,128)(2,1)S(1)}, bf16[2,9,256,256]{3,2,1,0:T(8,128)(2,1)S(1)}) custom-call(s32[8,2,2,9]{3,2,1,0:T(2,128)S(1)} %bitcast.5, bf16[32,256,256]{2,1,0:T(8,128)(2,1)S(1)} %all_to_all.10.noise_ref, bf16[9,8,256,256]{3,2,1,0:T(8,128)(2,1)} %factors_ref.1), custom_call_target="tpu_custom_call" | custom-call | flops 603979776 | bytes 524288 | tf_op jit(solution)/shard_map/pallas_call | solution.py:95
  65.6 5.7 %collective-permute-start = (s16[32,16,128]{2,1,0:T(8,128)(2,1)S(1)}, s16[32,16,128]{2,1,0:T(8,128)(2,1)S(1)}, u32[]{:S(2)}, u32[]{:S(2)}) collective-permute-start(s16[32,16,128]{2,1,0:T(8,128)(2,1)S(1)} %get-tuple-element.8), channel_id=1, source_target_pairs={{44,1},{1,44},{45,2},{2,45},{46,3},{3,46},{124,81},{81,124},{125,8... | collective-permute-start | bytes 393224 | tf_op jit(solution)/shard_map/ppermute | solution.py:267
  71.3 11.9 %shard_map.47 = s16[32,528,128]{2,1,0:T(8,128)(2,1)S(1)} custom-call(bf16[32,256,256]{2,1,0:T(8,128)(2,1)S(1)} %all_to_all.10.noise_ref, bf16[2,9,256,256]{3,2,1,0:T(8,128)(2,1)S(1)} %get-tuple-element.7.weights_ref), custom_call_target="tpu_custom_call" | custom-call | flops 9663676416 | bytes 8388608 | tf_op jit(solution)/shard_map/pallas_call | solution.py:159
  83.2 0.0 collective-permute-done
  83.3 0.1 add_dynamic-update-slice_fusion
  83.3 0.0 copy-start
  83.3 60.1 %all_to_all.11 = s16[32,528,128]{2,1,0:T(8,128)(2,1)S(1)} all-to-all(s16[32,528,128]{2,1,0:T(8,128)(2,1)S(1)} %add_dynamic-update-slice_fusion), channel_id=1, replica_groups={{0,4,40,44,80,84,120,124,32,36,72,76,112,116,24,28,64,68,104,108,16,20,..., dimensions={0} | all-to-all | bytes 8650752 | tf_op jit(solution)/shard_map/all_to_all | solution.py:272
  143.5 0.0 copy-done
  143.5 8.4 %shard_map.48 = f32[8,1024,256]{2,1,0:T(8,128)} custom-call(s16[8,4,528,128]{3,2,1,0:T(8,128)(2,1)S(1)} %bitcast.4, f32[5,1024]{1,0:T(8,128)S(1)} %copy-done), custom_call_target="tpu_custom_call" | custom-call | flops 20971520 | bytes 12582912 | tf_op jit(solution)/shard_map/pallas_call | solution.py:226
  (2 shorter events, 0.0 us)
Async XLA Ops:
  0.0 62.1 %copy-start.1 = (s32[9,8,2,2]{0,3,2,1:T(2,128)S(1)}, s32[9,8,2,2]{0,3,2,1:T(2,128)}, u32[]{:S(2)}) copy-start(s32[9,8,2,2]{0,3,2,1:T(2,128)} %param.6) | copy-start | bytes 3460
  65.6 17.6 %collective-permute-start = (s16[32,16,128]{2,1,0:T(8,128)(2,1)S(1)}, s16[32,16,128]{2,1,0:T(8,128)(2,1)S(1)}, u32[]{:S(2)}, u32[]{:S(2)}) collective-permute-start(s16[32,16,128]{2,1,0:T(8,128)(2,1)S(1)} %get-tuple-element.8), channel_id=1, source_target_pairs={{44,1},{1,44},{45,2},{2,45},{46,3},{3,46},{124,81},{81,124},{125,8... | collective-permute-start | bytes 393224 | tf_op jit(solution)/shard_map/ppermute | solution.py:267
  83.3 60.1 %copy-start = (f32[5,1024]{1,0:T(8,128)S(1)}, f32[5,1024]{1,0:T(8,128)}, u32[]{:S(2)}) copy-start(f32[5,1024]{1,0:T(8,128)} %lat_ref.1) | copy-start | bytes 61444

commit v4 on v3

--- a/solution.py
+++ b/solution.py
@@ -15,11 +15,11 @@
 
 
 def device_at(place):
-    return ((place // 8 + place // 2) % 4) * 8 + place % 8
+    return place // 8 * 8 + place % 4 * 2 + place // 4 % 2
 
 
 def place_of(device):
-    return ((device // 8 + 4 - device // 2 % 4) % 4) * 8 + device % 8
+    return device // 8 * 8 + device % 2 * 4 + device // 2 % 4
 
 
 def code(block):
@@ -118,7 +118,7 @@
     )(mask, noise, factors)
 
 
-def mix_kernel(noise_ref, weights_ref, coded_ref, powers, places):
+def mix_kernel(noise_ref, weights_ref, lat_ref, coded_ref, spread_ref, powers, places):
     parts, lags, width, _ = weights_ref.shape
     count, rows, _ = noise_ref.shape
     strip = rows // parts
@@ -133,6 +133,14 @@
     weights = [weights_ref.at[part, lag] for lag in range(lags)]
     lines = pl.ds(pl.multiple_of(part * strip, strip), strip)
     total = banded(places, noise_ref, weights, step * group, group, lines)
+    taps = spread_ref.shape[0]
+    start = pl.multiple_of((step * parts + part) * TILE, TILE)
+    empty = jnp.zeros((8 - taps, TILE), jnp.float32)
+    columns = jnp.concatenate([lat_ref[:, pl.ds(start, TILE)], empty], axis=0).T
+    for tap in range(taps):
+        spread_ref[tap, pl.ds(start, TILE), :] = jnp.broadcast_to(
+            columns[:, tap : tap + 1], (TILE, TILE)
+        )
     for g in range(group):
         block = total[g * strip : (g + 1) * strip]
         for half in range(halves):
@@ -151,17 +159,20 @@
             )
 
 
-def mix(noise, weights):
+def mix(noise, weights, lat_weights):
     count, rows, width = noise.shape
     parts, lags = weights.shape[:2]
     strip = rows // parts
     sent = rows * width // TILE + SIDE
     return pl.pallas_call(
         mix_kernel,
-        out_shape=jax.ShapeDtypeStruct((count, sent, TILE), jnp.int16),
+        out_shape=[
+            jax.ShapeDtypeStruct((count, sent, TILE), jnp.int16),
+            jax.ShapeDtypeStruct((*lat_weights.shape, TILE), jnp.float32),
+        ],
         grid=(count // GROUP, parts),
-        in_specs=[pl.BlockSpec(memory_space=pltpu.VMEM)] * 2,
-        out_specs=pl.BlockSpec(memory_space=pltpu.VMEM),
+        in_specs=[pl.BlockSpec(memory_space=pltpu.VMEM)] * 3,
+        out_specs=[pl.BlockSpec(memory_space=pltpu.VMEM)] * 2,
         scratch_shapes=[
             pltpu.VMEM((parts * GROUP, 8, TILE), jnp.int32),
             pltpu.SMEM((count + lags - 1,), jnp.int32),
@@ -172,26 +183,16 @@
             bytes_accessed=4 * count * rows * width,
             transcendentals=0,
         ),
-    )(noise, weights)
-
-
-def filter_kernel(parts, coded_ref, lat_ref, out_ref, padded, spread):
+    )(noise, weights, lat_weights)
+
+
+def filter_kernel(parts, coded_ref, spread_ref, out_ref, padded):
     shares, _, _ = coded_ref.shape
     rows, width = out_ref.shape
     halves = width // TILE
     held = rows // shares
     strip = held // parts
-    taps = spread.shape[0]
-
-    @pl.when(pl.program_id(0) == 0)
-    def _():
-        empty = jnp.zeros((8 - taps, TILE), jnp.float32)
-        for start in range(0, rows, TILE):
-            lines = slice(start, start + TILE)
-            columns = jnp.concatenate([lat_ref[:, lines], empty], axis=0).T
-            for tap in range(taps):
-                spread[tap, lines, :] = jnp.broadcast_to(columns[:, tap : tap + 1], (TILE, TILE))
-
+    taps = spread_ref.shape[0]
     for share in range(shares):
         side = coded_ref[share, halves * held :].astype(jnp.float32)
         for half in range(halves):
@@ -215,34 +216,33 @@
             total = None
             for tap in range(taps):
                 place = 8 - RIM + tap + start
-                term = spread[tap, start : start + strip] * padded[place : place + strip, lanes]
+                term = spread_ref[tap, start : start + strip] * padded[place : place + strip, lanes]
                 total = term if total is None else total + term
             out_ref[start : start + strip, lanes] = total
 
 
-def band_filter(coded, lat_weights, parts, width):
+def band_filter(coded, spread, parts, width):
     fields, shares, sent, _ = coded.shape
-    taps, rows = lat_weights.shape
+    rows = spread.shape[1]
     return pl.pallas_call(
         functools.partial(filter_kernel, parts),
         out_shape=jax.ShapeDtypeStruct((fields, rows, width), jnp.float32),
         grid=(fields,),
         in_specs=[
             pl.BlockSpec((None, shares, sent, TILE), lambda f: (f, 0, 0, 0)),
-            pl.BlockSpec((taps, rows), lambda f: (0, 0)),
+            pl.BlockSpec(memory_space=pltpu.VMEM),
         ],
         out_specs=pl.BlockSpec((None, rows, width), lambda f: (f, 0, 0)),
         scratch_shapes=[
             pltpu.VMEM((rows + 16, width), jnp.float32),
-            pltpu.VMEM((taps, rows, TILE), jnp.float32),
-        ],
-        compiler_params=pltpu.CompilerParams(vmem_limit_bytes=12 * 2**20),
+        ],
+        compiler_params=pltpu.CompilerParams(vmem_limit_bytes=10 * 2**20),
         cost_estimate=pl.CostEstimate(
             flops=10 * fields * rows * width,
             bytes_accessed=6 * fields * rows * width,
             transcendentals=0,
         ),
-    )(coded, lat_weights)
+    )(coded, spread)
 
 
 def per_device(noise, factors, tile_mask, lat_weights):
@@ -265,13 +265,13 @@
     )
     edges, weights = rim(tile_mask.transpose(1, 2, 3, 0), mine, factors, parts, shares)
     other = lax.ppermute(edges, ("lon", "lat"), joins)
-    coded = mix(mine, weights)
+    coded, spread = mix(mine, weights, lat_weights)
     own = SIDE - 3 * (width // TILE)
     side = jnp.concatenate([coded[:, -SIDE : own - SIDE], other[:, own:]], axis=1)
     coded = lax.dynamic_update_slice(coded, side, (0, coded.shape[1] - SIDE, 0))
     coded = lax.all_to_all(coded, "lon", 0, 0, axis_index_groups=groups, tiled=True)
     result_field = band_filter(
-        coded.reshape(fields, shares, -1, TILE), lat_weights, parts, width
+        coded.reshape(fields, shares, -1, TILE), spread, parts, width
     )
     return result_field.reshape(members, levels, rows, width)
 

time: 154 us -> 150 us (0.974); the launches traced: 152 us -> 150 us
  no operation moved by 1% of the time
where the time goes in v4:
time: 150 us
  blocking collectives  122 us (81%)
  Pallas kernels  22.9 us (15%)
  starting transfers between devices  4.69 us (3%)
    all_to_all x1, blocking collectives, per_device(): lax.all_to_all(noise.reshape(count, held, width), 'lon', 0, 0, axis_index...  62.1 us
    all_to_all x1, blocking collectives, per_device(): lax.all_to_all(coded, 'lon', 0, 0, axis_index_groups=groups, tiled=True)  59.7 us
    pallas_call x1, Pallas kernels, mix(): pl.pallas_call(mix_kernel, out_shape=[jax.ShapeDtypeStruct((count, sent,...  11.9 us
    pallas_call x1, Pallas kernels, band_filter(): pl.pallas_call(functools.partial(filter_kernel, parts), out_shape=jax.Sha...  7.48 us
    ppermute x1, starting transfers between devices, per_device(): other = lax.ppermute(edges, ('lon', 'lat'), joins)  4.69 us
    pallas_call x1, Pallas kernels, rim(): pl.pallas_call(functools.partial(rim_kernel, shares), out_shape=[jax.Shap...  3.51 us
  transfers between devices with their start and end apart: 1, of which 0 were waited for; matrix products, arithmetic and copies ran while one was open for 0% of the time, Pallas kernels for 8%

profile of v4, /device:TPU:1, one launch (start us, length us, event | category | flops | bytes accessed | tf_op | source)
XLA Modules:
  0.0 149.6 jit_solution(6783702573313158517)
XLA Ops:
  0.0 0.0 copy-start
  0.0 62.1 %all_to_all.10.noise_ref = bf16[32,256,256]{2,1,0:T(8,128)(2,1)S(1)} all-to-all(bf16[32,256,256]{2,1,0:T(8,128)(2,1)} %bitcast.6), channel_id=1, replica_groups={{0,8,16,24,4,12,20,28,32,40,48,56,36,44,52,60,64,72,80,88,68,76,84,92,9..., dimensions={0} | all-to-all | bytes 8388608 | tf_op jit(solution)/shard_map/all_to_all | solution.py:263
  62.1 0.0 copy-done
  62.1 0.0 copy-start.1
  62.1 3.5 %shard_map.46 = (s16[32,16,128]{2,1,0:T(8,128)(2,1)S(1)}, bf16[2,9,256,256]{3,2,1,0:T(8,128)(2,1)S(1)}) custom-call(s32[8,2,2,9]{3,2,1,0:T(2,128)S(1)} %bitcast.5, bf16[32,256,256]{2,1,0:T(8,128)(2,1)S(1)} %all_to_all.10.noise_ref, bf16[9,8,256,256]{3,2,1,0:T(8,128)(2,1)} %factors_ref.1), custom_call_target="tpu_custom_call" | custom-call | flops 603979776 | bytes 524288 | tf_op jit(solution)/shard_map/pallas_call | solution.py:95
  65.6 4.7 %collective-permute-start = (s16[32,16,128]{2,1,0:T(8,128)(2,1)S(1)}, s16[32,16,128]{2,1,0:T(8,128)(2,1)S(1)}, u32[]{:S(2)}, u32[]{:S(2)}) collective-permute-start(s16[32,16,128]{2,1,0:T(8,128)(2,1)S(1)} %get-tuple-element.11), channel_id=1, source_target_pairs={{24,1},{1,24},{25,2},{2,25},{26,3},{3,26},{28,5},{5,28},{29,6},{6,... | collective-permute-start | bytes 393224 | tf_op jit(solution)/shard_map/ppermute | solution.py:267
  70.3 0.0 copy-done.1
  70.3 11.9 %shard_map.47 = (s16[32,528,128]{2,1,0:T(8,128)(2,1)S(1)}, f32[5,1024,128]{2,1,0:T(8,128)S(1)}) custom-call(bf16[32,256,256]{2,1,0:T(8,128)(2,1)S(1)} %all_to_all.10.noise_ref, bf16[2,9,256,256]{3,2,1,0:T(8,128)(2,1)S(1)} %get-tuple-element.9.weights_ref, f32[5,1024]{1,0:T(8,128)S(1)} %copy-done.1), custom_call_target="tpu_custom_call" | custom-call | flops 9663676416 | bytes 8388608 | tf_op jit(solution)/shard_map/pallas_call | solution.py:167
  82.2 0.0 collective-permute-done
  82.3 0.1 add_dynamic-update-slice_fusion
  82.3 59.7 %all_to_all.11 = s16[32,528,128]{2,1,0:T(8,128)(2,1)S(1)} all-to-all(s16[32,528,128]{2,1,0:T(8,128)(2,1)S(1)} %add_dynamic-update-slice_fusion), channel_id=1, replica_groups={{0,8,16,24,4,12,20,28,32,40,48,56,36,44,52,60,64,72,80,88,68,76,84,92,9..., dimensions={0} | all-to-all | bytes 8650752 | tf_op jit(solution)/shard_map/all_to_all | solution.py:272
  142.1 7.5 %shard_map.48 = f32[8,1024,256]{2,1,0:T(8,128)} custom-call(s16[8,4,528,128]{3,2,1,0:T(8,128)(2,1)S(1)} %bitcast.4, f32[5,1024,128]{2,1,0:T(8,128)S(1)} %get-tuple-element.12.spread_ref), custom_call_target="tpu_custom_call" | custom-call | flops 20971520 | bytes 12582912 | tf_op jit(solution)/shard_map/pallas_call | solution.py:227
  (2 shorter events, 0.0 us)
Async XLA Ops:
  0.0 62.1 %copy-start = (s32[9,8,2,2]{0,3,2,1:T(2,128)S(1)}, s32[9,8,2,2]{0,3,2,1:T(2,128)}, u32[]{:S(2)}) copy-start(s32[9,8,2,2]{0,3,2,1:T(2,128)} %param.6) | copy-start | bytes 3460
  62.1 8.2 %copy-start.1 = (f32[5,1024]{1,0:T(8,128)S(1)}, f32[5,1024]{1,0:T(8,128)}, u32[]{:S(2)}) copy-start(f32[5,1024]{1,0:T(8,128)} %lat_ref.1) | copy-start | bytes 61444
  65.6 16.6 %collective-permute-start = (s16[32,16,128]{2,1,0:T(8,128)(2,1)S(1)}, s16[32,16,128]{2,1,0:T(8,128)(2,1)S(1)}, u32[]{:S(2)}, u32[]{:S(2)}) collective-permute-start(s16[32,16,128]{2,1,0:T(8,128)(2,1)S(1)} %get-tuple-element.11), channel_id=1, source_target_pairs={{24,1},{1,24},{25,2},{2,25},{26,3},{3,26},{28,5},{5,28},{29,6},{6,... | collective-permute-start | bytes 393224 | tf_op jit(solution)/shard_map/ppermute | solution.py:267

commit v5 on v4

--- a/solution.py
+++ b/solution.py
@@ -11,7 +11,7 @@
 RIM = 2
 TOP = 32767.0
 SIDE = 16
-GROUP = 8
+GROUP = 16
 
 
 def device_at(place):
@@ -23,9 +23,9 @@
 
 
 def code(block):
-    peak = jnp.maximum(jnp.max(jnp.abs(block), axis=0, keepdims=True), 2.0**-120)
+    peak = jnp.maximum(jnp.max(jnp.abs(block), axis=0, keepdims=True), 2.0**-110)
     power = jnp.ceil(jnp.log2(peak) + 1e-5)
-    return jnp.round(block * jnp.exp2(-power) * TOP).astype(jnp.int32), power.astype(jnp.int32)
+    return jnp.round(block * (jnp.exp2(-power) * TOP)).astype(jnp.int32), power.astype(jnp.int32)
 
 
 def fill_places(places, count, reach):
@@ -54,25 +54,29 @@
     tiles = width // TILE
     share = place_of(lax.axis_index("lon")) % shares
     last = share == shares - 1
+    order = [jnp.where(last, parts - 1 - part, part) for part in range(parts)]
     copies = [
         pltpu.make_async_copy(
-            factors_ref.at[:, share * parts + part], loaded.at[part], sems.at[part]
+            factors_ref.at[:, share * parts + order[index]], loaded.at[index], sems.at[index]
         )
-        for part in range(parts)
+        for index in range(parts)
     ]
     for copy in copies:
         copy.start()
     fill_places(places, count, lags // 2)
-    for part in range(parts):
-        copies[part].wait()
+
+    def mask_part(index, part):
+        copies[index].wait()
         for lag in range(lags):
             for a in range(tiles):
                 for b in range(tiles):
                     keep = mask_ref[share * parts + part, a, b, lag]
                     keep = keep.astype(jnp.float32).astype(jnp.bfloat16)
                     spot = (pl.ds(a * TILE, TILE), pl.ds(b * TILE, TILE))
-                    weights_ref[(part, lag, *spot)] = loaded[(part, lag, *spot)] * keep
-    weights = [weights_ref.at[jnp.where(last, parts - 1, 0), lag] for lag in range(lags)]
+                    weights_ref[(part, lag, *spot)] = loaded[(index, lag, *spot)] * keep
+
+    mask_part(0, order[0])
+    weights = [weights_ref.at[order[0], lag] for lag in range(lags)]
     line = pl.multiple_of(jnp.where(last, rows - SIDE, 0), SIDE)
     total = banded(places, noise_ref, weights, 0, count, pl.ds(line, SIDE))
     for g in range(count):
@@ -85,6 +89,8 @@
             codes.append(coded)
         empty = jnp.zeros((SIDE - 3 * len(codes), TILE), jnp.int32)
         side_ref[g] = jnp.concatenate([empty] + powers + codes, axis=0).astype(jnp.int16)
+    for index in range(1, parts):
+        mask_part(index, order[index])
 
 
 def rim(mask, noise, factors, parts, shares):
@@ -134,13 +140,15 @@
     lines = pl.ds(pl.multiple_of(part * strip, strip), strip)
     total = banded(places, noise_ref, weights, step * group, group, lines)
     taps = spread_ref.shape[0]
-    start = pl.multiple_of((step * parts + part) * TILE, TILE)
     empty = jnp.zeros((8 - taps, TILE), jnp.float32)
-    columns = jnp.concatenate([lat_ref[:, pl.ds(start, TILE)], empty], axis=0).T
-    for tap in range(taps):
-        spread_ref[tap, pl.ds(start, TILE), :] = jnp.broadcast_to(
-            columns[:, tap : tap + 1], (TILE, TILE)
-        )
+    pieces = spread_ref.shape[1] // TILE * group // (count * parts)
+    for piece in range(pieces):
+        start = pl.multiple_of(((step * parts + part) * pieces + piece) * TILE, TILE)
+        columns = jnp.concatenate([lat_ref[:, pl.ds(start, TILE)], empty], axis=0).T
+        for tap in range(taps):
+            spread_ref[tap, pl.ds(start, TILE), :] = jnp.broadcast_to(
+                columns[:, tap : tap + 1], (TILE, TILE)
+            )
     for g in range(group):
         block = total[g * strip : (g + 1) * strip]
         for half in range(halves):

time: 150 us -> 149 us (level)
  no operation moved by 1% of the time
where the time goes in v5:
time: 149 us
  blocking collectives  122 us (82%)
  Pallas kernels  22.2 us (15%)
  starting transfers between devices  4.65 us (3%)
    all_to_all x1, blocking collectives, per_device(): lax.all_to_all(noise.reshape(count, held, width), 'lon', 0, 0, axis_index...  62.1 us
    all_to_all x1, blocking collectives, per_device(): lax.all_to_all(coded, 'lon', 0, 0, axis_index_groups=groups, tiled=True)  59.7 us
    pallas_call x1, Pallas kernels, mix(): pl.pallas_call(mix_kernel, out_shape=[jax.ShapeDtypeStruct((count, sent,...  11.3 us
    pallas_call x1, Pallas kernels, band_filter(): pl.pallas_call(functools.partial(filter_kernel, parts), out_shape=jax.Sha...  7.48 us
    ppermute x1, starting transfers between devices, per_device(): other = lax.ppermute(edges, ('lon', 'lat'), joins)  4.65 us
    pallas_call x1, Pallas kernels, rim(): pl.pallas_call(functools.partial(rim_kernel, shares), out_shape=[jax.Shap...  3.38 us
  transfers between devices with their start and end apart: 1, of which 0 were waited for; matrix products, arithmetic and copies ran while one was open for 0% of the time, Pallas kernels for 8%

profile of v5, /device:TPU:1, one launch (start us, length us, event | category | flops | bytes accessed | tf_op | source)
XLA Modules:
  0.0 148.8 jit_solution(10167033039391117568)
XLA Ops:
  0.0 0.0 copy-start
  0.0 62.1 %all_to_all.10.noise_ref = bf16[32,256,256]{2,1,0:T(8,128)(2,1)S(1)} all-to-all(bf16[32,256,256]{2,1,0:T(8,128)(2,1)} %bitcast.6), channel_id=1, replica_groups={{0,8,16,24,4,12,20,28,32,40,48,56,36,44,52,60,64,72,80,88,68,76,84,92,9..., dimensions={0} | all-to-all | bytes 8388608 | tf_op jit(solution)/shard_map/all_to_all | solution.py:271
  62.1 0.0 copy-done
  62.1 0.0 copy-start.1
  62.1 3.4 %shard_map.46 = (s16[32,16,128]{2,1,0:T(8,128)(2,1)S(1)}, bf16[2,9,256,256]{3,2,1,0:T(8,128)(2,1)S(1)}) custom-call(s32[8,2,2,9]{3,2,1,0:T(2,128)S(1)} %bitcast.5, bf16[32,256,256]{2,1,0:T(8,128)(2,1)S(1)} %all_to_all.10.noise_ref, bf16[9,8,256,256]{3,2,1,0:T(8,128)(2,1)} %factors_ref.1), custom_call_target="tpu_custom_call" | custom-call | flops 603979776 | bytes 524288 | tf_op jit(solution)/shard_map/pallas_call | solution.py:101
  65.5 4.7 %collective-permute-start = (s16[32,16,128]{2,1,0:T(8,128)(2,1)S(1)}, s16[32,16,128]{2,1,0:T(8,128)(2,1)S(1)}, u32[]{:S(2)}, u32[]{:S(2)}) collective-permute-start(s16[32,16,128]{2,1,0:T(8,128)(2,1)S(1)} %get-tuple-element.11), channel_id=1, source_target_pairs={{24,1},{1,24},{25,2},{2,25},{26,3},{3,26},{28,5},{5,28},{29,6},{6,... | collective-permute-start | bytes 393224 | tf_op jit(solution)/shard_map/ppermute | solution.py:275
  70.2 0.0 copy-done.1
  70.2 11.3 %shard_map.47 = (s16[32,528,128]{2,1,0:T(8,128)(2,1)S(1)}, f32[5,1024,128]{2,1,0:T(8,128)S(1)}) custom-call(bf16[32,256,256]{2,1,0:T(8,128)(2,1)S(1)} %all_to_all.10.noise_ref, bf16[2,9,256,256]{3,2,1,0:T(8,128)(2,1)S(1)} %get-tuple-element.9.weights_ref, f32[5,1024]{1,0:T(8,128)S(1)} %copy-done.1), custom_call_target="tpu_custom_call" | custom-call | flops 9663676416 | bytes 8388608 | tf_op jit(solution)/shard_map/pallas_call | solution.py:175
  81.5 0.0 collective-permute-done
  81.5 0.1 add_dynamic-update-slice_fusion
  81.6 59.7 %all_to_all.11 = s16[32,528,128]{2,1,0:T(8,128)(2,1)S(1)} all-to-all(s16[32,528,128]{2,1,0:T(8,128)(2,1)S(1)} %add_dynamic-update-slice_fusion), channel_id=1, replica_groups={{0,8,16,24,4,12,20,28,32,40,48,56,36,44,52,60,64,72,80,88,68,76,84,92,9..., dimensions={0} | all-to-all | bytes 8650752 | tf_op jit(solution)/shard_map/all_to_all | solution.py:280
  141.3 7.5 %shard_map.48 = f32[8,1024,256]{2,1,0:T(8,128)} custom-call(s16[8,4,528,128]{3,2,1,0:T(8,128)(2,1)S(1)} %bitcast.4, f32[5,1024,128]{2,1,0:T(8,128)S(1)} %get-tuple-element.12.spread_ref), custom_call_target="tpu_custom_call" | custom-call | flops 20971520 | bytes 12582912 | tf_op jit(solution)/shard_map/pallas_call | solution.py:235
  (2 shorter events, 0.0 us)
Async XLA Ops:
  0.0 62.1 %copy-start = (s32[9,8,2,2]{0,3,2,1:T(2,128)S(1)}, s32[9,8,2,2]{0,3,2,1:T(2,128)}, u32[]{:S(2)}) copy-start(s32[9,8,2,2]{0,3,2,1:T(2,128)} %param.6) | copy-start | bytes 3460
  62.1 8.1 %copy-start.1 = (f32[5,1024]{1,0:T(8,128)S(1)}, f32[5,1024]{1,0:T(8,128)}, u32[]{:S(2)}) copy-start(f32[5,1024]{1,0:T(8,128)} %lat_ref.1) | copy-start | bytes 61444
  65.5 16.0 %collective-permute-start = (s16[32,16,128]{2,1,0:T(8,128)(2,1)S(1)}, s16[32,16,128]{2,1,0:T(8,128)(2,1)S(1)}, u32[]{:S(2)}, u32[]{:S(2)}) collective-permute-start(s16[32,16,128]{2,1,0:T(8,128)(2,1)S(1)} %get-tuple-element.11), channel_id=1, source_target_pairs={{24,1},{1,24},{25,2},{2,25},{26,3},{3,26},{28,5},{5,28},{29,6},{6,... | collective-permute-start | bytes 393224 | tf_op jit(solution)/shard_map/ppermute | solution.py:275

commit v6 on v5

--- a/solution.py
+++ b/solution.py
@@ -15,11 +15,11 @@
 
 
 def device_at(place):
-    return place // 8 * 8 + place % 4 * 2 + place // 4 % 2
+    return place % 4 * 8 + place // 8 * 2 + place // 4 % 2
 
 
 def place_of(device):
-    return device // 8 * 8 + device % 2 * 4 + device // 2 % 4
+    return device // 2 % 4 * 8 + device % 2 * 4 + device // 8
 
 
 def code(block):

time: 149 us -> 148 us (level)
  no operation moved by 1% of the time
where the time goes in v6:
time: 148 us
  blocking collectives  121 us (82%)
  Pallas kernels  22.2 us (15%)
  starting transfers between devices  4.65 us (3%)
    all_to_all x1, blocking collectives, per_device(): lax.all_to_all(noise.reshape(count, held, width), 'lon', 0, 0, axis_index...  62.1 us
    all_to_all x1, blocking collectives, per_device(): lax.all_to_all(coded, 'lon', 0, 0, axis_index_groups=groups, tiled=True)  58.9 us
    pallas_call x1, Pallas kernels, mix(): pl.pallas_call(mix_kernel, out_shape=[jax.ShapeDtypeStruct((count, sent,...  11.3 us
    pallas_call x1, Pallas kernels, band_filter(): pl.pallas_call(functools.partial(filter_kernel, parts), out_shape=jax.Sha...  7.48 us
    ppermute x1, starting transfers between devices, per_device(): other = lax.ppermute(edges, ('lon', 'lat'), joins)  4.65 us
    pallas_call x1, Pallas kernels, rim(): pl.pallas_call(functools.partial(rim_kernel, shares), out_shape=[jax.Shap...  3.38 us
  transfers between devices with their start and end apart: 1, of which 0 were waited for; matrix products, arithmetic and copies ran while one was open for 0% of the time, Pallas kernels for 8%

profile of v6, /device:TPU:1, one launch (start us, length us, event | category | flops | bytes accessed | tf_op | source)
XLA Modules:
  0.0 148.0 jit_solution(10883195809754671258)
XLA Ops:
  0.0 0.0 copy-start
  0.0 62.1 %all_to_all.10.noise_ref = bf16[32,256,256]{2,1,0:T(8,128)(2,1)S(1)} all-to-all(bf16[32,256,256]{2,1,0:T(8,128)(2,1)} %bitcast.6), channel_id=1, replica_groups={{0,32,64,96,4,36,68,100,8,40,72,104,12,44,76,108,16,48,80,112,20,52,84,..., dimensions={0} | all-to-all | bytes 8388608 | tf_op jit(solution)/shard_map/all_to_all | solution.py:271
  62.1 0.0 copy-done
  62.1 0.0 copy-start.1
  62.1 3.4 %shard_map.46 = (s16[32,16,128]{2,1,0:T(8,128)(2,1)S(1)}, bf16[2,9,256,256]{3,2,1,0:T(8,128)(2,1)S(1)}) custom-call(s32[8,2,2,9]{3,2,1,0:T(2,128)S(1)} %bitcast.5, bf16[32,256,256]{2,1,0:T(8,128)(2,1)S(1)} %all_to_all.10.noise_ref, bf16[9,8,256,256]{3,2,1,0:T(8,128)(2,1)} %factors_ref.1), custom_call_target="tpu_custom_call" | custom-call | flops 603979776 | bytes 524288 | tf_op jit(solution)/shard_map/pallas_call | solution.py:101
  65.5 4.7 %collective-permute-start = (s16[32,16,128]{2,1,0:T(8,128)(2,1)S(1)}, s16[32,16,128]{2,1,0:T(8,128)(2,1)S(1)}, u32[]{:S(2)}, u32[]{:S(2)}) collective-permute-start(s16[32,16,128]{2,1,0:T(8,128)(2,1)S(1)} %get-tuple-element.11), channel_id=1, source_target_pairs={{96,1},{1,96},{97,2},{2,97},{98,3},{3,98},{100,5},{5,100},{101,6},... | collective-permute-start | bytes 393224 | tf_op jit(solution)/shard_map/ppermute | solution.py:275
  70.2 0.0 copy-done.1
  70.2 11.3 %shard_map.47 = (s16[32,528,128]{2,1,0:T(8,128)(2,1)S(1)}, f32[5,1024,128]{2,1,0:T(8,128)S(1)}) custom-call(bf16[32,256,256]{2,1,0:T(8,128)(2,1)S(1)} %all_to_all.10.noise_ref, bf16[2,9,256,256]{3,2,1,0:T(8,128)(2,1)S(1)} %get-tuple-element.9.weights_ref, f32[5,1024]{1,0:T(8,128)S(1)} %copy-done.1), custom_call_target="tpu_custom_call" | custom-call | flops 9663676416 | bytes 8388608 | tf_op jit(solution)/shard_map/pallas_call | solution.py:175
  81.5 0.0 collective-permute-done
  81.6 0.1 add_dynamic-update-slice_fusion
  81.6 58.9 %all_to_all.11 = s16[32,528,128]{2,1,0:T(8,128)(2,1)S(1)} all-to-all(s16[32,528,128]{2,1,0:T(8,128)(2,1)S(1)} %add_dynamic-update-slice_fusion), channel_id=1, replica_groups={{0,32,64,96,4,36,68,100,8,40,72,104,12,44,76,108,16,48,80,112,20,52,84,..., dimensions={0} | all-to-all | bytes 8650752 | tf_op jit(solution)/shard_map/all_to_all | solution.py:280
  140.5 7.5 %shard_map.48 = f32[8,1024,256]{2,1,0:T(8,128)} custom-call(s16[8,4,528,128]{3,2,1,0:T(8,128)(2,1)S(1)} %bitcast.4, f32[5,1024,128]{2,1,0:T(8,128)S(1)} %get-tuple-element.12.spread_ref), custom_call_target="tpu_custom_call" | custom-call | flops 20971520 | bytes 12582912 | tf_op jit(solution)/shard_map/pallas_call | solution.py:235
  (2 shorter events, 0.0 us)
Async XLA Ops:
  0.0 62.1 %copy-start = (s32[9,8,2,2]{0,3,2,1:T(2,128)S(1)}, s32[9,8,2,2]{0,3,2,1:T(2,128)}, u32[]{:S(2)}) copy-start(s32[9,8,2,2]{0,3,2,1:T(2,128)} %param.6) | copy-start | bytes 3460
  62.1 8.1 %copy-start.1 = (f32[5,1024]{1,0:T(8,128)S(1)}, f32[5,1024]{1,0:T(8,128)}, u32[]{:S(2)}) copy-start(f32[5,1024]{1,0:T(8,128)} %lat_ref.1) | copy-start | bytes 61444
  65.5 16.0 %collective-permute-start = (s16[32,16,128]{2,1,0:T(8,128)(2,1)S(1)}, s16[32,16,128]{2,1,0:T(8,128)(2,1)S(1)}, u32[]{:S(2)}, u32[]{:S(2)}) collective-permute-start(s16[32,16,128]{2,1,0:T(8,128)(2,1)S(1)} %get-tuple-element.11), channel_id=1, source_target_pairs={{96,1},{1,96},{97,2},{2,97},{98,3},{3,98},{100,5},{5,100},{101,6},... | collective-permute-start | bytes 393224 | tf_op jit(solution)/shard_map/ppermute | solution.py:275

commit v7 on v6

--- a/solution.py
+++ b/solution.py
@@ -11,7 +11,7 @@
 RIM = 2
 TOP = 32767.0
 SIDE = 16
-GROUP = 16
+GROUP = 32
 
 
 def device_at(place):
@@ -185,7 +185,7 @@
             pltpu.VMEM((parts * GROUP, 8, TILE), jnp.int32),
             pltpu.SMEM((count + lags - 1,), jnp.int32),
         ],
-        compiler_params=pltpu.CompilerParams(vmem_limit_bytes=16 * 2**20),
+        compiler_params=pltpu.CompilerParams(vmem_limit_bytes=24 * 2**20),
         cost_estimate=pl.CostEstimate(
             flops=2 * lags * count * rows * width * width,
             bytes_accessed=4 * count * rows * width,

time: 148 us -> 148 us (level)
  no operation moved by 1% of the time
where the time goes in v7:
time: 148 us
  blocking collectives  121 us (82%)
  Pallas kernels  22.1 us (15%)
  starting transfers between devices  4.65 us (3%)
    all_to_all x1, blocking collectives, per_device(): lax.all_to_all(noise.reshape(count, held, width), 'lon', 0, 0, axis_index...  62.1 us
    all_to_all x1, blocking collectives, per_device(): lax.all_to_all(coded, 'lon', 0, 0, axis_index_groups=groups, tiled=True)  58.9 us
    pallas_call x1, Pallas kernels, mix(): pl.pallas_call(mix_kernel, out_shape=[jax.ShapeDtypeStruct((count, sent,...  11.2 us
    pallas_call x1, Pallas kernels, band_filter(): pl.pallas_call(functools.partial(filter_kernel, parts), out_shape=jax.Sha...  7.48 us
    ppermute x1, starting transfers between devices, per_device(): other = lax.ppermute(edges, ('lon', 'lat'), joins)  4.65 us
    pallas_call x1, Pallas kernels, rim(): pl.pallas_call(functools.partial(rim_kernel, shares), out_shape=[jax.Shap...  3.38 us
  transfers between devices with their start and end apart: 1, of which 0 were waited for; matrix products, arithmetic and copies ran while one was open for 0% of the time, Pallas kernels for 8%

profile of v7, /device:TPU:1, one launch (start us, length us, event | category | flops | bytes accessed | tf_op | source)
XLA Modules:
  0.0 147.9 jit_solution(11727287719881959117)
XLA Ops:
  0.0 0.0 copy-start
  0.0 62.1 %all_to_all.10.noise_ref = bf16[32,256,256]{2,1,0:T(8,128)(2,1)S(1)} all-to-all(bf16[32,256,256]{2,1,0:T(8,128)(2,1)} %bitcast.6), channel_id=1, replica_groups={{0,32,64,96,4,36,68,100,8,40,72,104,12,44,76,108,16,48,80,112,20,52,84,..., dimensions={0} | all-to-all | bytes 8388608 | tf_op jit(solution)/shard_map/all_to_all | solution.py:271
  62.1 0.0 copy-done
  62.1 0.0 copy-start.1
  62.1 3.4 %shard_map.46 = (s16[32,16,128]{2,1,0:T(8,128)(2,1)S(1)}, bf16[2,9,256,256]{3,2,1,0:T(8,128)(2,1)S(1)}) custom-call(s32[8,2,2,9]{3,2,1,0:T(2,128)S(1)} %bitcast.5, bf16[32,256,256]{2,1,0:T(8,128)(2,1)S(1)} %all_to_all.10.noise_ref, bf16[9,8,256,256]{3,2,1,0:T(8,128)(2,1)} %factors_ref.1), custom_call_target="tpu_custom_call" | custom-call | flops 603979776 | bytes 524288 | tf_op jit(solution)/shard_map/pallas_call | solution.py:101
  65.5 4.7 %collective-permute-start = (s16[32,16,128]{2,1,0:T(8,128)(2,1)S(1)}, s16[32,16,128]{2,1,0:T(8,128)(2,1)S(1)}, u32[]{:S(2)}, u32[]{:S(2)}) collective-permute-start(s16[32,16,128]{2,1,0:T(8,128)(2,1)S(1)} %get-tuple-element.11), channel_id=1, source_target_pairs={{96,1},{1,96},{97,2},{2,97},{98,3},{3,98},{100,5},{5,100},{101,6},... | collective-permute-start | bytes 393224 | tf_op jit(solution)/shard_map/ppermute | solution.py:275
  70.2 0.0 copy-done.1
  70.2 11.2 %shard_map.47 = (s16[32,528,128]{2,1,0:T(8,128)(2,1)S(1)}, f32[5,1024,128]{2,1,0:T(8,128)S(1)}) custom-call(bf16[32,256,256]{2,1,0:T(8,128)(2,1)S(1)} %all_to_all.10.noise_ref, bf16[2,9,256,256]{3,2,1,0:T(8,128)(2,1)S(1)} %get-tuple-element.9.weights_ref, f32[5,1024]{1,0:T(8,128)S(1)} %copy-done.1), custom_call_target="tpu_custom_call" | custom-call | flops 9663676416 | bytes 8388608 | tf_op jit(solution)/shard_map/pallas_call | solution.py:175
  81.4 0.0 collective-permute-done
  81.5 0.1 add_dynamic-update-slice_fusion
  81.5 58.9 %all_to_all.11 = s16[32,528,128]{2,1,0:T(8,128)(2,1)S(1)} all-to-all(s16[32,528,128]{2,1,0:T(8,128)(2,1)S(1)} %add_dynamic-update-slice_fusion), channel_id=1, replica_groups={{0,32,64,96,4,36,68,100,8,40,72,104,12,44,76,108,16,48,80,112,20,52,84,..., dimensions={0} | all-to-all | bytes 8650752 | tf_op jit(solution)/shard_map/all_to_all | solution.py:280
  140.4 7.5 %shard_map.48 = f32[8,1024,256]{2,1,0:T(8,128)} custom-call(s16[8,4,528,128]{3,2,1,0:T(8,128)(2,1)S(1)} %bitcast.4, f32[5,1024,128]{2,1,0:T(8,128)S(1)} %get-tuple-element.12.spread_ref), custom_call_target="tpu_custom_call" | custom-call | flops 20971520 | bytes 12582912 | tf_op jit(solution)/shard_map/pallas_call | solution.py:235
  (2 shorter events, 0.0 us)
Async XLA Ops:
  0.0 62.1 %copy-start = (s32[9,8,2,2]{0,3,2,1:T(2,128)S(1)}, s32[9,8,2,2]{0,3,2,1:T(2,128)}, u32[]{:S(2)}) copy-start(s32[9,8,2,2]{0,3,2,1:T(2,128)} %param.6) | copy-start | bytes 3460
  62.1 8.1 %copy-start.1 = (f32[5,1024]{1,0:T(8,128)S(1)}, f32[5,1024]{1,0:T(8,128)}, u32[]{:S(2)}) copy-start(f32[5,1024]{1,0:T(8,128)} %lat_ref.1) | copy-start | bytes 61444
  65.5 15.9 %collective-permute-start = (s16[32,16,128]{2,1,0:T(8,128)(2,1)S(1)}, s16[32,16,128]{2,1,0:T(8,128)(2,1)S(1)}, u32[]{:S(2)}, u32[]{:S(2)}) collective-permute-start(s16[32,16,128]{2,1,0:T(8,128)(2,1)S(1)} %get-tuple-element.11), channel_id=1, source_target_pairs={{96,1},{1,96},{97,2},{2,97},{98,3},{3,98},{100,5},{5,100},{101,6},... | collective-permute-start | bytes 393224 | tf_op jit(solution)/shard_map/ppermute | solution.py:275
